TPU v7x, 256 devices: a whole 4x4x8 slice. The times are simulated.
256 devices in a mesh: branch: 16 (over x, z_hi), seq: 16 (over y, z_lo, core).
Axes of the slice: x: 4, y: 4, z: 8 (z_hi: 4, z_lo: 2; z = z_hi * 2 + z_lo), core: 2. Of those that a mesh axis runs over, the one named last changes fastest.
Arguments:
- query_proj: bfloat16 [16, 4096, 3072], P('branch', 'seq'), may hold values from -6 to 6
- key_proj: bfloat16 [16, 4096, 3072], P('branch', 'seq'), may hold values from -6 to 6
- value_proj: bfloat16 [16, 4096, 3072], P('branch', 'seq'), may hold values from -6 to 6
- learn_rate: bfloat16 [16, 4096, 48], P('branch', 'seq'), may hold values from 0.0099487305 to 0.29882812
- norm_gain: float32 [48, 64], P('seq'), may hold values from 0.25 to 1.75
- norm_shift: float32 [48, 64], P('seq'), may hold values from -3 to 3
- start_offset: int32 [16], P('branch'), may hold values from 0 to 4095
- owner_map: int32 [16], replicated, may hold values from 0 to 15, as said below
- first_weight: float32 [16, 48, 64, 256], P('branch', 'seq'), may hold values from -0.75 to 0.75
- first_bias: float32 [16, 48, 256], P('branch', 'seq'), may hold values from -3 to 3
- second_weight: float32 [16, 48, 256, 64], P('branch', 'seq'), may hold values from -0.375 to 0.375
- second_bias: float32 [16, 48, 64], P('branch', 'seq'), may hold values from -3 to 3
Outputs:
- layer_out: bfloat16 [16, 4096, 3072], P('branch', 'seq')
Inputs may be any that keep to these rules, and one draw needn't show every extreme that they name: `owner_map`: each entry names a branch.
All inputs are finite; a program needn't handle non-finite values.
Results may differ from a plain program's by a relative error of at most 0.0019.
Values may be sent and summed in bfloat16 or wider, within the bound.
No kernel may reach another device: no remote copies, remote signals or barrier semaphores. Data moves between devices by JAX's collectives and lax.ppermute only.
A program may use at most 128 MiB of HBM per device.

v0:
```python
import jax
import jax.numpy as jnp
from jax import lax
from jax.sharding import PartitionSpec as P

MB = 64


HIGHEST = lax.Precision.HIGHEST


def rotate(values_in, positions):
    half = values_in.shape[-1] // 2
    freqs = jnp.exp(-jnp.log(10000.0) * jnp.arange(half, dtype=jnp.float32) / half)
    angles = positions.astype(jnp.float32)[:, None] * freqs[None, :]
    cosine = jnp.cos(angles)[:, None, :]
    sine = jnp.sin(angles)[:, None, :]
    first = values_in[..., :half]
    second = values_in[..., half:]
    return jnp.concatenate([first * cosine - second * sine, first * sine + second * cosine], -1)


def norm_out(hidden, gain, shift):
    center = hidden - jnp.mean(hidden, -1, keepdims=True)
    spread = jnp.mean(center * center, -1, keepdims=True)
    return center * lax.rsqrt(spread + 1e-06) * gain[:, None, :] + shift[:, None, :]


def inner_model(params, inputs, gain, shift):
    weight_one, bias_one, weight_two, bias_two = params
    hidden = (
        jnp.einsum("hbe,hef->hbf", inputs, weight_one, precision=HIGHEST) + bias_one[:, None, :]
    )
    active = jax.nn.gelu(hidden, approximate=True)
    result = (
        jnp.einsum("hbf,hfe->hbe", active, weight_two, precision=HIGHEST) + bias_two[:, None, :]
    )
    return norm_out(result, gain, shift)


def inner_loss(params, inputs, target, rates, gain, shift):
    error = inner_model(params, inputs, gain, shift) - target
    return 0.5 * jnp.sum(rates[..., None] * error * error) / inputs.shape[1]


def inner_step(params, block, gain, shift):
    query, keyed, valued, rates = block
    grads = jax.grad(inner_loss)(params, keyed, valued - keyed, rates, gain, shift)
    params = tuple((param - grad for param, grad in zip(params, grads)))
    return (params, query + inner_model(params, query, gain, shift))


def run_heads(params, query, keyed, valued, rates, gain, shift, block_len):
    blocks = query.shape[1] // block_len

    def split_blocks(array):
        shaped = array.reshape((array.shape[0], blocks, block_len) + array.shape[2:])
        return jnp.moveaxis(shaped, 1, 0)

    def advance(carry, block):
        return inner_step(carry, block, gain, shift)

    params, results = lax.scan(
        advance,
        params,
        (split_blocks(query), split_blocks(keyed), split_blocks(valued), split_blocks(rates)),
        unroll=4,
    )
    results = jnp.moveaxis(results, 0, 1)
    return results.reshape(query.shape)


def body(
    query_proj,
    key_proj,
    value_proj,
    learn_rate,
    norm_gain,
    norm_shift,
    start_offset,
    owner_map,
    first_weight,
    first_bias,
    second_weight,
    second_bias,
):
    groups = lax.axis_size("seq")
    local_heads = first_weight.shape[1]
    head_dim = first_weight.shape[2]
    tok_local = query_proj.shape[1]
    source = owner_map[lax.axis_index("branch")]
    pieces_in = (first_weight, first_bias, second_weight, second_bias)
    empty = tuple((jnp.zeros(piece.shape[1:], jnp.float32) for piece in pieces_in))
    pieces = (
        lax.all_gather(first_weight, "branch", axis=0, tiled=True),
        lax.all_gather(first_bias, "branch", axis=0, tiled=True),
        lax.all_gather(second_weight, "branch", axis=0, tiled=True),
        lax.all_gather(second_bias, "branch", axis=0, tiled=True),
    )
    count = pieces[0].shape[0]
    hits = jnp.arange(count, dtype=jnp.int32) == source
    picked = []
    for total, piece in zip(empty, pieces):
        shaped_hits = hits.reshape((count,) + (1,) * (piece.ndim - 1))
        picked.append(jnp.sum(jnp.where(shaped_hits, piece, 0.0), 0))
    weight_one, bias_one, weight_two, bias_two = tuple(picked)

    def heads_view(array):
        return array.reshape(tok_local, groups, local_heads, head_dim)

    query_all, key_all, value_all, rate_all = (
        lax.all_to_all(heads_view(query_proj), "seq", split_axis=1, concat_axis=0, tiled=True),
        lax.all_to_all(heads_view(key_proj), "seq", split_axis=1, concat_axis=0, tiled=True),
        lax.all_to_all(heads_view(value_proj), "seq", split_axis=1, concat_axis=0, tiled=True),
        lax.all_to_all(
            learn_rate.reshape(tok_local, groups, local_heads),
            "seq",
            split_axis=1,
            concat_axis=0,
            tiled=True,
        ),
    )
    total_tokens = query_all.shape[0]
    positions = start_offset[0] + jnp.arange(total_tokens, dtype=jnp.int32)
    query = rotate(
        query_all.reshape(total_tokens, local_heads, head_dim).astype(jnp.float32), positions
    )
    keyed = rotate(
        key_all.reshape(total_tokens, local_heads, head_dim).astype(jnp.float32), positions
    )
    valued = value_all.reshape(total_tokens, local_heads, head_dim).astype(jnp.float32)
    rates = jnp.swapaxes(rate_all.reshape(total_tokens, local_heads).astype(jnp.float32), 0, 1)
    params = (weight_one, bias_one, weight_two, bias_two)
    result = run_heads(
        params,
        jnp.swapaxes(query, 0, 1),
        jnp.swapaxes(keyed, 0, 1),
        jnp.swapaxes(valued, 0, 1),
        rates,
        norm_gain,
        norm_shift,
        MB,
    )
    result = jnp.swapaxes(result.astype(jnp.bfloat16), 0, 1).reshape(
        total_tokens, 1, local_heads * head_dim
    )
    merged = lax.all_to_all(result, "seq", split_axis=0, concat_axis=1, tiled=True)
    return merged.reshape(1, tok_local, groups * local_heads * head_dim)


def solution(mesh):
    return jax.shard_map(
        body,
        mesh=mesh,
        in_specs=(
            P("branch", "seq", None),
            P("branch", "seq", None),
            P("branch", "seq", None),
            P("branch", "seq", None),
            P("seq", None),
            P("seq", None),
            P("branch"),
            P(),
            P("branch", "seq", None, None),
            P("branch", "seq", None),
            P("branch", "seq", None, None),
            P("branch", "seq", None),
        ),
        out_specs=P("branch", "seq", None),
        check_vma=False,
    )
```

profile of v0, /device:TPU:1, one launch (start us, length us, event | category | flops | bytes accessed | tf_op | source)
XLA Modules:
  0.0 715.0 jit_solution(17065506497187289303)
XLA Ops:
  8.6 7.3 %all-to-all-start.1 = ((bf16[256,16,3]{0,2,1:T(4,128)(2,1)}), bf16[256,16,3]{0,2,1:T(4,128)(2,1)S(1)}, u32[]{:S(2)}, u32[]{:S(2)}) async-start(bf16[256,16,3]{0,2,1:T(4,128)(2,1)} %reshape.383), calls=%async_computation.1 | async-start | bytes 65536 | tf_op jit(solution)/shard_map/all_to_all | solution.py:115
  21.8 3.9 all-to-all-start
  27.2 26.2 %all-to-all-done = bf16[256,16,3,64]{0,3,2,1:T(8,128)(2,1)S(1)} async-done(((bf16[256,16,3,64]{0,3,2,1:T(8,128)(2,1)}), bf16[256,16,3,64]{0,3,2,1:T(8,128)(2,1)S(1)}, u32[]{:S(2)}, u32[]{:S(2)}) %all-to-all-start) | async-done | bytes 1572896 | tf_op jit(solution)/shard_map/all_to_all | solution.py:113
  53.4 4.4 all-to-all-start.3
  65.2 34.1 %all-to-all-done.3 = bf16[256,16,3,64]{0,3,2,1:T(8,128)(2,1)S(1)} async-done(((bf16[256,16,3,64]{0,3,2,1:T(8,128)(2,1)}), bf16[256,16,3,64]{0,3,2,1:T(8,128)(2,1)S(1)}, u32[]{:S(2)}, u32[]{:S(2)}) %all-to-all-start.3) | async-done | bytes 1572896 | tf_op jit(solution)/shard_map/all_to_all | solution.py:112
  99.3 4.7 all-to-all-start.2
  104.6 57.9 %all_gather.15 = f32[16,3,64]{2,1,0:T(4,128)S(1)} all-gather(f32[1,3,64]{2,1,0:T(4,128)S(1)} %copy.75), channel_id=1, replica_groups=mesh['branch'=16,'seq'=16] {'branch'}, dimensions={0}, use_global_device_ids=true | all-gather | bytes 13056 | tf_op jit(solution)/shard_map/all_gather | solution.py:98
  162.5 33.3 %all_gather.13 = f32[16,3,256]{2,1,0:T(4,128)S(1)} all-gather(f32[1,3,256]{2,1,0:T(4,128)S(1)} %copy.74), channel_id=1, replica_groups=mesh['branch'=16,'seq'=16] {'branch'}, dimensions={0}, use_global_device_ids=true | all-gather | bytes 52224 | tf_op jit(solution)/shard_map/all_gather | solution.py:96
  207.4 4.0 multiply_subtract_fusion
  213.7 6.1 reshape.381
  219.8 4.3 reshape.392
  230.0 6.1 reshape.408
  240.7 391.2 %while.21 = (s32[]{:T(128)}, f32[3,64,256]{2,1,0:T(8,128)S(1)}, f32[3,256]{1,0:T(4,128)S(1)}, f32[3,256,64]{1,2,0:T(8,128)S(1)}, f32[3,64]{1,0:T(4,128)S(1)}, /*...) while((s32[]{:T(128)}, f32[3,64,256]{2,1,0:T(8,128)S(1)}, ...), condition=%wide.region_37.38_spmd, body=%wide.region_4.37_spmd.sunk | while | flops 1069210368 | bytes 20090096 | solution.py:63
  342.5 3.4 constant_dynamic-slice_fusion.21
  391.7 3.4 constant_dynamic-slice_fusion.21
  538.1 3.4 constant_dynamic-slice_fusion.21
  587.1 3.2 constant_dynamic-slice_fusion.21
  632.0 4.3 copy.86
  636.2 3.4 convert_element_type.82
  640.2 3.9 reduce
  647.2 3.3 reshape.422
  650.5 37.7 %all_to_all.51 = bf16[16,2,24576]{2,1,0:T(2,128)(2,1)S(1)} all-to-all(bf16[16,2,24576]{2,1,0:T(2,128)(2,1)} %reshape.422), channel_id=1, replica_groups=mesh['branch'=16,'seq'=16] {'seq'}, dimensions={0} | all-to-all | bytes 3145728 | tf_op jit(solution)/shard_map/all_to_all | solution.py:147
  688.2 7.3 %reshape.423 = bf16[4096,1,192]{2,1,0:T(2,128)(2,1)} reshape(bf16[16,2,24576]{2,1,0:T(2,128)(2,1)S(1)} %all_to_all.51) | data formatting | bytes 3145728
  695.5 9.9 %copy.88 = bf16[4096,1,192]{0,2,1:T(8,128)(2,1)S(1)} copy(bf16[4096,1,192]{2,1,0:T(2,128)(2,1)} %reshape.423) | data formatting | bytes 3145728 | tf_op jit(solution)/shard_map/all_to_all | solution.py:147
  (1667 shorter events, 419.3 us)
Async XLA Ops:
  6.5 229.6 %all-gather.5.cloned.1.call-start = ((), (), s32[]{:S(2)}) async-start(), calls=%async_computation.6 | async-start | bytes 3342336 | tf_op jit(solution)/shard_map/all_gather | solution.py:97
  8.6 13.1 %all-to-all-start.1 = ((bf16[256,16,3]{0,2,1:T(4,128)(2,1)}), bf16[256,16,3]{0,2,1:T(4,128)(2,1)S(1)}, u32[]{:S(2)}, u32[]{:S(2)}) async-start(bf16[256,16,3]{0,2,1:T(4,128)(2,1)} %reshape.383), calls=%async_computation.1 | async-start | bytes 65536 | tf_op jit(solution)/shard_map/all_to_all | solution.py:115
  18.6 7.1 copy-start.3
  21.8 31.6 %all-to-all-start = ((bf16[256,16,3,64]{0,3,2,1:T(8,128)(2,1)}), bf16[256,16,3,64]{0,3,2,1:T(8,128)(2,1)S(1)}, u32[]{:S(2)}, u32[]{:S(2)}) async-start(bf16[256,16,3,64]{0,3,2,1:T(8,128)(2,1)} %bitcast.22), calls=%async_computation | async-start | bytes 3145728 | tf_op jit(solution)/shard_map/all_to_all | solution.py:113
  53.4 45.9 %all-to-all-start.3 = ((bf16[256,16,3,64]{0,3,2,1:T(8,128)(2,1)}), bf16[256,16,3,64]{0,3,2,1:T(8,128)(2,1)S(1)}, u32[]{:S(2)}, u32[]{:S(2)}) async-start(bf16[256,16,3,64]{0,3,2,1:T(8,128)(2,1)} %bitcast.41), calls=%async_computation.3 | async-start | bytes 3145728 | tf_op jit(solution)/shard_map/all_to_all | solution.py:112
  57.8 4.1 copy-start.6
  57.8 180.7 %all-gather.3.cloned.1.call-start = ((), (), s32[]{:S(2)}) async-start(), calls=%async_computation.5 | async-start | bytes 3342336 | tf_op jit(solution)/shard_map/all_gather | solution.py:95
  62.4 42.1 %copy-start.4 = (f32[1,3,256]{2,0,1:T(1,128)S(1)}, f32[1,3,256]{2,0,1:T(1,128)}, u32[]{:S(2)}) copy-start(f32[1,3,256]{2,0,1:T(1,128)} %param.23) | copy-start | bytes 9220
  62.4 42.2 %copy-start.5 = (f32[1,3,64]{2,0,1:T(1,128)S(1)}, f32[1,3,64]{2,0,1:T(1,128)}, u32[]{:S(2)}) copy-start(f32[1,3,64]{2,0,1:T(1,128)} %param.25) | copy-start | bytes 2308
  99.3 97.5 %copy-start = (bf16[256,16,3,64]{0,3,2,1:T(8,128)(2,1)}, bf16[256,16,3,64]{0,3,2,1:T(8,128)(2,1)S(1)}, u32[]{:S(2)}) copy-start(bf16[256,16,3,64]{0,3,2,1:T(8,128)(2,1)S(1)} %all-to-all-done.3) | copy-start | bytes 4718596
  99.3 124.8 %all-to-all-start.2 = ((bf16[256,16,3,64]{0,3,2,1:T(8,128)(2,1)}), bf16[256,16,3,64]{0,3,2,1:T(8,128)(2,1)}, u32[]{:S(2)}, u32[]{:S(2)}) async-start(bf16[256,16,3,64]{0,3,2,1:T(8,128)(2,1)} %bitcast.35), calls=%async_computation.2 | async-start | bytes 3145728 | tf_op jit(solution)/shard_map/all_to_all | solution.py:114
  238.4 2.3 copy-start.1
  238.4 2.3 copy-start.2
Sparse Core Ops, SparseCore 0:
  9.8 82.1 all-gather.4
  94.5 68.2 all-gather.2
where the time goes:
time: 718 us; the launch traced here: 715 us
  local copies, waits for them, and re-layouts  191 us (27%)
  matrix products  183 us (25%)
  blocking collectives  129 us (18%)
  other arithmetic  106 us (15%)
  waiting for transfers between devices  64.8 us (9%)
  starting transfers between devices  20.3 us (3%)
  between operations  14.3 us (2%)
    dot_general x256, matrix products, inner_model(): jnp.einsum('hbf,hfe->hbe', active, weight_two, precision=HIGHEST)  112 us
    slice x48, local copies, waits for them, and re-layouts, run_heads(): lax.scan(advance, params, (split_blocks(query), split_blocks(keyed), spli...  98.5 us
    dot_general x192, matrix products, inner_model(): jnp.einsum('hbe,hef->hbf', inputs, weight_one, precision=HIGHEST)  71.6 us
    all_gather x1, blocking collectives, body(): lax.all_gather(second_bias, 'branch', axis=0, tiled=True)  57.9 us
    all_to_all x1, blocking collectives, body(): lax.all_to_all(result, 'seq', split_axis=0, concat_axis=1, tiled=True)  37.7 us
    all_to_all x1, waiting for transfers between devices, body(): lax.all_to_all(heads_view(query_proj), 'seq', split_axis=1, concat_axis=0...  34.1 us
    all_gather x1, blocking collectives, body(): lax.all_gather(first_bias, 'branch', axis=0, tiled=True)  33.3 us
    all_to_all x1, waiting for transfers between devices, body(): lax.all_to_all(heads_view(key_proj), 'seq', split_axis=1, concat_axis=0,...  26.2 us
  transfers between devices with their start and end apart: 6, of which 3 were waited for; matrix products, arithmetic and copies ran while one was open for 8% of the time, Pallas kernels for 0%

commit v1 on v0

v1 whole, which is shorter than its diff:
```python
import jax
import jax.numpy as jnp
from jax import lax
from jax.experimental import pallas as pl
from jax.experimental.pallas import tpu as pltpu
from jax.sharding import PartitionSpec as P

f32, bf16 = jnp.float32, jnp.bfloat16
C0 = 0.7978845608028654
C1 = 0.044715
MB = 64


def split(x):
    hi = x.astype(bf16)
    return hi, (x - hi.astype(f32)).astype(bf16)


def stack4(hi, lo, axis):
    return jnp.concatenate([hi, lo, hi, lo], axis)


def dot(a, b):
    return jnp.dot(a, b, preferred_element_type=f32)


def dot_nt(a, b):
    return lax.dot_general(a, b, (((1,), (1,)), ((), ())), preferred_element_type=f32)


def ttt_kernel(x_ref, cos_ref, sin_ref, gain_ref, shift_ref,
               w1_in, c1_in, w2_in, c2_in, out_ref,
               w1_ref, c1_ref, w2_ref, c2_ref, qprev_ref, yprev_ref):
    nh = w1_ref.shape[0]
    nb = x_ref.shape[0]
    rows = nh * 64
    w1_ref[...] = w1_in[...]
    c1_ref[...] = c1_in[...]
    w2_ref[...] = w2_in[...]
    c2_ref[...] = c2_in[...]
    qprev_ref[...] = jnp.zeros_like(qprev_ref)
    yprev_ref[...] = jnp.zeros_like(yprev_ref)
    low = lax.broadcasted_iota(jnp.int32, (64, 128), 1) < 64
    low1 = lax.broadcasted_iota(jnp.int32, (1, 128), 1) < 64

    heads = range(nh)

    def tokmajor(x):
        xt = jnp.transpose(jnp.concatenate([x, x], 0))
        hi, lo = split(xt)
        return hi, lo

    def forward(xps):
        xs = [jnp.concatenate(tokmajor(x), 1) for x in xps]
        w1s = [stack4(*split(w1_ref[h]), 0) for h in heads]
        hid = [dot(xs[h], w1s[h]) + c1_ref[h] for h in heads]
        h2 = [x * x for x in hid]
        th = [jnp.tanh(hid[h] * (h2[h] * (C0 * C1) + C0)) for h in heads]
        hh = [0.5 * x for x in hid]
        aa = [split(hh[h] * th[h] + hh[h]) for h in heads]
        ww = [split(w2_ref[h]) for h in heads]
        z4 = [dot_nt(jnp.concatenate(ww[h], 0), jnp.concatenate(aa[h], 0)) for h in heads]
        z = [(z[:64, :128] + z[64:, 128:]) + (z[64:, :128] + z[:64, 128:]) + c2_ref[h] for h, z in enumerate(z4)]
        c = [z[h] - jnp.mean(z[h], 0, keepdims=True) for h in heads]
        rstd = [lax.rsqrt(jnp.mean(c[h] * c[h], 0, keepdims=True) + 1e-06) for h in heads]
        return hid, h2, th, hh, aa, ww, c, rstd

    def step(xp, pq, bc, rate, xdup, even):
        hid, h2, th, hh, aa, ww, c, rstd = forward(xp)
        lo_k = 0 if even else 64
        sl = slice(lo_k, lo_k + 64)
        dz, y = [], []
        for h in heads:
            gain = gain_ref[h]
            y.append(c[h] * rstd[h] * gain + pq[h])
            g2c = gain * gain * c[h]
            m2 = jnp.mean(g2c, 0, keepdims=True)
            m3 = jnp.mean(g2c * c[h], 0, keepdims=True)
            m4 = jnp.mean(bc[h] * c[h], 0, keepdims=True)
            s = rstd[h] * rate[h]
            e = rstd[h] * rstd[h] * (rstd[h] * m3 + m4)
            dz.append(s * ((g2c - m2) * rstd[h] + bc[h] - c[h] * e))
        lhs = []
        for h in heads:
            dzh, dzl = tokmajor(dz[h])
            lhs.append(jnp.concatenate([dzh[sl], dzl[sl]], 1))
        da = [dot(lhs[h], stack4(*ww[h], 0)) for h in heads]
        gp = []
        for h in heads:
            hk, h2k, thk, hhk = hid[h][sl], h2[h][sl], th[h][sl], hh[h][sl]
            du = h2k * (3 * C0 * C1) + C0
            gp.append((0.5 * thk + 0.5) + (hhk * du) * (1.0 - thk * thk))
        dh = [da[h] * gp[h] for h in heads]
        dw1 = [dot(xdup[h], stack4(*split(dh[h]), 0)) for h in heads]
        dw2 = []
        for h in heads:
            d = dz[h] + pltpu.roll(dz[h], 64, 1)
            dw2.append(dot(jnp.concatenate(split(d), 1), stack4(aa[h][0][sl], aa[h][1][sl], 0)))
        for h in heads:
            w2_ref[h] = w2_ref[h] - dw2[h]
            c2_ref[h] = c2_ref[h] - jnp.sum(dz[h], 1, keepdims=True)
            w1_ref[h] = w1_ref[h] - dw1[h]
            c1_ref[h] = c1_ref[h] - jnp.sum(dh[h], 0, keepdims=True)
        return y

    def rot(x, cs, sn):
        a, b = x[:32], x[32:]
        return jnp.concatenate([a * cs - b * sn, a * sn + b * cs], 0)

    def block(b, _):
        for tile in range(2):
            ts = slice(tile * 128, tile * 128 + 128)
            cs = cos_ref[b, :, ts]
            sn = sin_ref[b, :, ts]
            ks, qs, ps, bcs, rts, xds = [], [], [], [], [], []
            rates = x_ref[b, 3 * rows:3 * rows + 16, ts].astype(f32) * (1.0 / MB)
            for h in heads:
                q = rot(x_ref[b, h * 64:h * 64 + 64, ts].astype(f32), cs, sn)
                k = rot(x_ref[b, rows + h * 64:rows + h * 64 + 64, ts].astype(f32), cs, sn)
                v = x_ref[b, 2 * rows + h * 64:2 * rows + h * 64 + 64, ts].astype(f32)
                bb = gain_ref[h] * (shift_ref[h] - (v - k))
                bc = bb - jnp.mean(bb, 0, keepdims=True)
                kr = pltpu.roll(k, 64, 1)
                ks.append(k)
                qs.append(q)
                bcs.append(bc)
                rts.append(rates[h:h + 1])
                e_hi, e_lo = split(jnp.where(low, k, kr))
                o_hi, o_lo = split(jnp.where(low, kr, k))
                xds.append((jnp.concatenate([e_hi, e_lo], 1), jnp.concatenate([o_hi, o_lo], 1)))
            pb = jnp.maximum(b - 1, 0) if tile == 0 else b
            pts = slice(128, 256) if tile == 0 else slice(0, 128)
            qp = [qprev_ref[h] for h in heads]
            y = step([jnp.where(low, ks[h], qp[h]) for h in heads], [qp[h] + shift_ref[h] for h in heads], bcs,
                     [jnp.where(low1, rts[h], 0.0) for h in heads], [x[0] for x in xds], True)
            for h in heads:
                hs = slice(h * 64, h * 64 + 64)
                out_ref[pb, hs, pts] = jnp.where(low, yprev_ref[h], y[h]).astype(bf16)
            y = step([jnp.where(low, qs[h], ks[h]) for h in heads], [qs[h] + shift_ref[h] for h in heads], bcs,
                     [jnp.where(low1, 0.0, rts[h]) for h in heads], [x[1] for x in xds], False)
            for h in heads:
                yprev_ref[h] = y[h]
                qprev_ref[h] = qs[h]
        return 0

    lax.fori_loop(0, nb, block, 0)
    qp = [qprev_ref[h] for h in heads]
    c, rstd = forward(qp)[-2:]
    for h in heads:
        hs = slice(h * 64, h * 64 + 64)
        y = c[h] * rstd[h] * gain_ref[h] + qp[h] + shift_ref[h]
        out_ref[nb - 1, hs, 128:256] = jnp.where(low, yprev_ref[h], y).astype(bf16)


def ttt(x, cos, sin, gain, shift, w1, c1, w2, c2):
    nh = w1.shape[0]
    return pl.pallas_call(
        ttt_kernel,
        out_shape=jax.ShapeDtypeStruct((x.shape[0], nh * 64, x.shape[2]), bf16),
        in_specs=[pl.BlockSpec(memory_space=pltpu.VMEM)] * 9,
        out_specs=pl.BlockSpec(memory_space=pltpu.VMEM),
        scratch_shapes=[
            pltpu.VMEM((nh, 64, 256), f32),
            pltpu.VMEM((nh, 1, 256), f32),
            pltpu.VMEM((nh, 64, 256), f32),
            pltpu.VMEM((nh, 64, 128), f32),
            pltpu.VMEM((nh, 64, 128), f32),
            pltpu.VMEM((nh, 64, 128), f32),
        ],
        compiler_params=pltpu.CompilerParams(vmem_limit_bytes=48 * 1024 * 1024),
    )(x, cos, sin, gain, shift, w1, c1, w2, c2)


def tables(off, n):
    half = 32
    freqs = jnp.exp(-jnp.log(10000.0) * jnp.arange(half, dtype=f32) / half)
    pos = (off + jnp.arange(n, dtype=jnp.int32)).astype(f32)
    ang = pos.reshape(n // 256, 1, 256) * freqs[None, :, None]
    return jnp.cos(ang), jnp.sin(ang)


def body(
    query_proj,
    key_proj,
    value_proj,
    learn_rate,
    norm_gain,
    norm_shift,
    start_offset,
    owner_map,
    first_weight,
    first_bias,
    second_weight,
    second_bias,
):
    groups = lax.axis_size("seq")
    nh, tok = first_weight.shape[1], query_proj.shape[1]
    source = owner_map[lax.axis_index("branch")]

    w2t = jnp.swapaxes(second_weight[0], 1, 2)
    packed = jnp.concatenate([first_weight[0], w2t], 0).reshape(16, 24, 256)
    held = lax.all_to_all(packed, "branch", split_axis=0, concat_axis=0, tiled=True)
    picked = jnp.take(held, owner_map, axis=0)
    own = lax.all_to_all(picked, "branch", split_axis=0, concat_axis=0, tiled=True)
    own = own.reshape(2 * nh, 64, 256)
    biases = lax.all_gather(jnp.concatenate([first_bias[0], second_bias[0]], 1), "branch")
    bias = lax.dynamic_index_in_dim(biases, source, 0, keepdims=False)
    w1, w2 = own[:nh], own[nh:]
    w2 = w2 - jnp.mean(w2, 1, keepdims=True)
    c1, c2 = bias[:, :256], bias[:, 256:]
    c2 = c2 - jnp.mean(c2, 1, keepdims=True)

    def column(x):
        return jnp.broadcast_to(x[:, :, None], x.shape + (128,))

    def by_group(x):
        return x[0].T.reshape(groups, x.shape[2] // groups, tok)

    rates = jnp.pad(by_group(learn_rate), ((0, 0), (0, 16 - nh), (0, 0)))
    x = jnp.concatenate([by_group(query_proj), by_group(key_proj), by_group(value_proj), rates], 1)
    x = lax.all_to_all(x, "seq", split_axis=0, concat_axis=0, tiled=True)
    cos, sin = tables(start_offset[0], groups * tok)
    y = ttt(x, cos, sin, column(norm_gain), column(norm_shift), w1, c1[:, None, :], w2, column(c2))
    y = lax.all_to_all(y, "seq", split_axis=0, concat_axis=0, tiled=True)
    return y.reshape(groups * nh * 64, tok).T[None]


def solution(mesh):
    return jax.shard_map(
        body,
        mesh=mesh,
        in_specs=(
            P("branch", "seq", None),
            P("branch", "seq", None),
            P("branch", "seq", None),
            P("branch", "seq", None),
            P("seq", None),
            P("seq", None),
            P("branch"),
            P(),
            P("branch", "seq", None, None),
            P("branch", "seq", None),
            P("branch", "seq", None, None),
            P("branch", "seq", None),
        ),
        out_specs=P("branch", "seq", None),
        check_vma=False,
    )
```

time: 718 us -> 240 us (0.33)
  matrix products: 183 us -> 0 us
  local copies, waits for them, and re-layouts: 191 us -> 9.58 us
  other arithmetic: 106 us -> 9.72 us
  Pallas kernels: 0 us -> 62.9 us
  waiting for transfers between devices: 64.8 us -> 17.2 us
  blocking collectives: 129 us -> 114 us
  between operations: 14.3 us -> 2.77 us
    dot_general x448 -> x0, matrix products: 183 us -> none  [the longest x256 112 us: inner_model(): jnp.einsum('hbf,hfe->hbe', active, weight_two, precision=HIGHEST)]
    slice x48 -> x2, local copies, waits for them, and re-layouts: 98.5 us -> 0.03 us  [the longest x1 0.03 us: body(): w1, w2 = (own[:nh], own[nh:])]
    reduce_sum x324 -> x2, other arithmetic: 68.8 us -> 0.14 us  [the longest x1 0.11 us: body(): c2 = c2 - jnp.mean(c2, 1, keepdims=True)]
    pallas_call x0 -> x1, Pallas kernels: none -> 62.9 us  [ttt(): pl.pallas_call(ttt_kernel, out_shape=jax.ShapeDtypeStruct((x.shape[0], nh...]
    all_to_all x4 -> x3, waiting for transfers between devices: 63.4 us -> 17.2 us  [the longest x1 13.3 us: body(): lax.all_to_all(packed, 'branch', split_axis=0, concat_axis=0, tiled=True)]
    reshape x9 -> x2, local copies, waits for them, and re-layouts: 25 us -> 3.1 us  [the longest x1 1.73 us: body(): return y.reshape(groups * nh * 64, tok).T[None]]
    unnamed x23 -> x14, local copies, waits for them, and re-layouts: 20.9 us -> 0.03 us
    while x192 -> x0, local copies, waits for them, and re-layouts: 18.9 us -> none
  transfers between devices with their start and end apart: 6 -> 3, of which waited for: 3 -> 2; matrix products, arithmetic and copies ran while one was open for 8% -> 6% of each run, Pallas kernels for 0% -> 0%
where the time goes in v1:
time: 240 us; the launch traced here: 239 us
  blocking collectives  114 us (48%)
  Pallas kernels  62.9 us (26%)
  starting transfers between devices  23.5 us (10%)
  waiting for transfers between devices  17.2 us (7%)
  other arithmetic  9.72 us (4%)
  local copies, waits for them, and re-layouts  9.58 us (4%)
  between operations  2.77 us (1%)
    all_gather x1, blocking collectives, body(): lax.all_gather(jnp.concatenate([first_bias[0], second_bias[0]], 1), 'bran...  79 us
    pallas_call x1, Pallas kernels, ttt(): pl.pallas_call(ttt_kernel, out_shape=jax.ShapeDtypeStruct((x.shape[0], nh...  62.9 us
    all_to_all x1, blocking collectives, body(): y = lax.all_to_all(y, 'seq', split_axis=0, concat_axis=0, tiled=True)  34.8 us
    all_to_all x1, waiting for transfers between devices, body(): lax.all_to_all(packed, 'branch', split_axis=0, concat_axis=0, tiled=True)  13.3 us
    all_to_all x1, starting transfers between devices, body(): lax.all_to_all(packed, 'branch', split_axis=0, concat_axis=0, tiled=True)  11.6 us
    all_to_all x1, starting transfers between devices, body(): x = lax.all_to_all(x, 'seq', split_axis=0, concat_axis=0, tiled=True)  8.4 us
    transpose x3, local copies, waits for them, and re-layouts, by_group(): return x[0].T.reshape(groups, x.shape[2] // groups, tok)  4.97 us
  transfers between devices with their start and end apart: 3, of which 2 were waited for; matrix products, arithmetic and copies ran while one was open for 6% of the time, Pallas kernels for 0%

profile of v1, /device:TPU:1, one launch (start us, length us, event | category | flops | bytes accessed | tf_op | source)
XLA Modules:
  0.0 239.5 jit_solution(12491163188622140420)
XLA Ops:
  0.0 1.9 pad_maximum_fusion
  1.9 11.6 %all-to-all-start.1 = ((f32[16,24,256]{2,1,0:T(8,128)}), f32[16,24,256]{2,1,0:T(8,128)S(1)}, u32[]{:S(2)}, u32[]{:S(2)}) async-start(f32[16,24,256]{2,1,0:T(8,128)} %bitcast.15), calls=%async_computation.1 | async-start | bytes 786432 | tf_op jit(solution)/shard_map/all_to_all | solution.py:202
  13.5 0.7 compare_select_fusion
  14.2 0.7 compare_and_fusion
  14.8 13.3 %all-to-all-done.1 = f32[16,24,256]{2,1,0:T(8,128)S(1)} async-done(((f32[16,24,256]{2,1,0:T(8,128)}), f32[16,24,256]{2,1,0:T(8,128)S(1)}, u32[]{:S(2)}, u32[]{:S(2)}) %all-to-all-start.1) | async-done | bytes 393248 | tf_op jit(solution)/shard_map/all_to_all | solution.py:202
  28.2 0.6 gather_fusion
  28.8 0.8 broadcast_select_fusion
  29.6 3.6 %all-to-all-start.2 = ((f32[16,24,256]{2,1,0:T(8,128)}), f32[16,24,256]{2,1,0:T(8,128)S(1)}, u32[]{:S(2)}, u32[]{:S(2)}) async-start(f32[16,24,256]{2,1,0:T(8,128)} %broadcast_select_fusion), calls=%async_computation.2 | async-start | bytes 786432 | tf_op jit(solution)/shard_map/all_to_all | solution.py:204
  33.2 1.4 reshape.55
  34.5 0.7 copy.23
  35.2 1.7 copy.22
  36.9 2.6 %copy.21 = bf16[3072,256]{1,0:T(8,128)(2,1)} copy(bf16[3072,256]{0,1:T(8,128)(2,1)} %bitcast.48) | data formatting | bytes 3145728 | tf_op jit(solution)/shard_map/transpose | solution.py:217
  39.5 3.5 %fusion.1 = bf16[16,592,256]{2,1,0:T(8,128)(2,1)} fusion(bf16[16,3,256]{2,1,0:T(4,128)(2,1)} %reshape.55, bf16[16,192,256]{2,1,0:T(8,128)(2,1)S(1)} %bitcast.40, bf16[16,192,256]{2,1,0:T(8,128)(2,1)S(1)} %bitcast.41, bf16[16,192,256]{2,1,0:T(8,128)(2,1)} %bitcast.42), kind=kLoop, calls=%fused_computation.3 | loop fusion | flops 24248320 | bytes 9592832 | tf_op jit(solution)/shard_map/concatenate | solution.py:220
  43.0 3.8 %all-to-all-done.2 = f32[16,24,256]{2,1,0:T(8,128)S(1)} async-done(((f32[16,24,256]{2,1,0:T(8,128)}), f32[16,24,256]{2,1,0:T(8,128)S(1)}, u32[]{:S(2)}, u32[]{:S(2)}) %all-to-all-start.2) | async-done | bytes 393248 | tf_op jit(solution)/shard_map/all_to_all | solution.py:204
  46.9 8.4 %all-to-all-start = ((bf16[16,592,256]{2,1,0:T(8,128)(2,1)}), bf16[16,592,256]{2,1,0:T(8,128)(2,1)}, u32[]{:S(2)}, u32[]{:S(2)}) async-start(bf16[16,592,256]{2,1,0:T(8,128)(2,1)} %fusion.1), calls=%async_computation | async-start | bytes 9699328 | tf_op jit(solution)/shard_map/all_to_all | solution.py:221
  55.3 0.6 dynamic_slice.7
  58.5 79.0 %all-gather.1 = f32[16,3,320]{2,1,0:T(4,128)S(1)} all-gather(f32[1,3,320]{2,1,0:T(4,128)S(1)} %maximum_bitcast_fusion), channel_id=2, replica_groups=mesh['branch'=16,'seq'=16] {'branch'}, dimensions={0}, use_global_device_ids=true | all-gather | bytes 65280 | tf_op jit(solution)/shard_map/all_gather | solution.py:206
  137.5 0.1 slice_reduce_fusion
  137.7 1.9 multiply_sine_fusion
  139.7 0.1 broadcast_in_dim.22.gain_ref
  139.9 0.1 broadcast_in_dim.45.c2_in
  140.0 62.9 %shard_map.118 = bf16[16,192,256]{2,1,0:T(8,128)(2,1)S(1)} custom-call(bf16[16,592,256]{2,1,0:T(8,128)(2,1)} %all-to-all-done.x_ref, f32[16,32,256]{2,1,0:T(8,128)S(1)} %get-tuple-element.8.cos_ref, f32[16,32,256]{2,1,0:T(8,128)S(1)} %get-tuple-element.7.sin_ref, f32[3,64,128]{2,1,0:T(8,128)S(1)} %broadcast_in_dim.22.gain_ref, ...), custom_call_target="tpu_custom_call" | custom-call | tf_op jit(solution)/shard_map/pallas_call | solution.py:157
  202.9 34.8 %all_to_all.20 = bf16[16,192,256]{2,1,0:T(8,128)(2,1)S(1)} all-to-all(bf16[16,192,256]{2,1,0:T(8,128)(2,1)S(1)} %shard_map.118), channel_id=1, replica_groups=mesh['branch'=16,'seq'=16] {'seq'}, dimensions={0} | all-to-all | bytes 3145728 | tf_op jit(solution)/shard_map/all_to_all | solution.py:224
  237.7 1.7 copy.24
  (29 shorter events, 0.3 us)
Async XLA Ops:
  0.0 34.5 %copy-start = (bf16[1,256,3072]{2,1,0:T(8,128)(2,1)S(1)}, bf16[1,256,3072]{2,1,0:T(8,128)(2,1)}, u32[]{:S(2)}) copy-start(bf16[1,256,3072]{2,1,0:T(8,128)(2,1)} %param.14) | copy-start | bytes 4718596
  1.9 26.3 %all-to-all-start.1 = ((f32[16,24,256]{2,1,0:T(8,128)}), f32[16,24,256]{2,1,0:T(8,128)S(1)}, u32[]{:S(2)}, u32[]{:S(2)}) async-start(f32[16,24,256]{2,1,0:T(8,128)} %bitcast.15), calls=%async_computation.1 | async-start | bytes 786432 | tf_op jit(solution)/shard_map/all_to_all | solution.py:202
  29.6 17.3 %all-to-all-start.2 = ((f32[16,24,256]{2,1,0:T(8,128)}), f32[16,24,256]{2,1,0:T(8,128)S(1)}, u32[]{:S(2)}, u32[]{:S(2)}) async-start(f32[16,24,256]{2,1,0:T(8,128)} %broadcast_select_fusion), calls=%async_computation.2 | async-start | bytes 786432 | tf_op jit(solution)/shard_map/all_to_all | solution.py:204
  43.0 12.3 %copy-start.5 = (s32[16]{0:T(128)S(1)}, s32[16]{0:T(128)}, u32[]{:S(2)}) copy-start(s32[16]{0:T(128)} %param.19) | copy-start | bytes 196
  43.0 14.8 %copy-start.4 = (f32[1,3,64]{2,0,1:T(1,128)S(1)}, f32[1,3,64]{2,0,1:T(1,128)}, u32[]{:S(2)}) copy-start(f32[1,3,64]{2,0,1:T(1,128)} %param.23) | copy-start | bytes 2308
  43.0 14.8 %copy-start.1 = (f32[1,3,256]{2,0,1:T(1,128)S(1)}, f32[1,3,256]{2,0,1:T(1,128)}, u32[]{:S(2)}) copy-start(f32[1,3,256]{2,0,1:T(1,128)} %param.21) | copy-start | bytes 9220
  43.0 96.7 %copy-start.2 = (f32[3,64]{1,0:T(4,128)S(1)}, f32[3,64]{1,0:T(4,128)}, u32[]{:S(2)}) copy-start(f32[3,64]{1,0:T(4,128)} %param.16) | copy-start | bytes 2308
  43.0 96.8 %copy-start.3 = (f32[3,64]{1,0:T(4,128)S(1)}, f32[3,64]{1,0:T(4,128)}, u32[]{:S(2)}) copy-start(f32[3,64]{1,0:T(4,128)} %param.17) | copy-start | bytes 2308
  46.9 92.8 %all-to-all-start = ((bf16[16,592,256]{2,1,0:T(8,128)(2,1)}), bf16[16,592,256]{2,1,0:T(8,128)(2,1)}, u32[]{:S(2)}, u32[]{:S(2)}) async-start(bf16[16,592,256]{2,1,0:T(8,128)(2,1)} %fusion.1), calls=%async_computation | async-start | bytes 9699328 | tf_op jit(solution)/shard_map/all_to_all | solution.py:221

commit v2 on v1

--- a/solution.py
+++ b/solution.py
@@ -29,21 +29,26 @@
 
 
 def ttt_kernel(x_ref, cos_ref, sin_ref, gain_ref, shift_ref,
-               w1_in, c1_in, w2_in, c2_in, out_ref,
+               own_ref, out_ref,
                w1_ref, c1_ref, w2_ref, c2_ref, qprev_ref, yprev_ref):
     nh = w1_ref.shape[0]
+    heads = range(nh)
     nb = x_ref.shape[0]
     rows = nh * 64
-    w1_ref[...] = w1_in[...]
-    c1_ref[...] = c1_in[...]
-    w2_ref[...] = w2_in[...]
-    c2_ref[...] = c2_in[...]
+    for h in heads:
+        hl = slice(h * 256, h * 256 + 256)
+        for i in range(8):
+            w1_ref[h, i * 8:i * 8 + 8] = own_ref[i, :, hl]
+        w2 = jnp.concatenate([own_ref[8 + i, :, hl] for i in range(8)], 0)
+        w2_ref[h] = w2 - jnp.mean(w2, 0, keepdims=True)
+        bias = own_ref[0, :, nh * 256:nh * 256 + 128]
+        c1_ref[h] = jnp.concatenate([bias[h:h + 1], bias[nh + h:nh + h + 1]], 1)
+        c2 = bias[2 * nh + h // 2:2 * nh + h // 2 + 1, h % 2 * 64:h % 2 * 64 + 64]
+        c2_ref[h] = jnp.transpose(jnp.broadcast_to(c2 - jnp.mean(c2), (128, 64)))
     qprev_ref[...] = jnp.zeros_like(qprev_ref)
     yprev_ref[...] = jnp.zeros_like(yprev_ref)
     low = lax.broadcasted_iota(jnp.int32, (64, 128), 1) < 64
     low1 = lax.broadcasted_iota(jnp.int32, (1, 128), 1) < 64
-
-    heads = range(nh)
 
     def tokmajor(x):
         xt = jnp.transpose(jnp.concatenate([x, x], 0))
@@ -152,12 +157,12 @@
         out_ref[nb - 1, hs, 128:256] = jnp.where(low, yprev_ref[h], y).astype(bf16)
 
 
-def ttt(x, cos, sin, gain, shift, w1, c1, w2, c2):
-    nh = w1.shape[0]
+def ttt(x, cos, sin, gain, shift, own):
+    nh = gain.shape[0]
     return pl.pallas_call(
         ttt_kernel,
         out_shape=jax.ShapeDtypeStruct((x.shape[0], nh * 64, x.shape[2]), bf16),
-        in_specs=[pl.BlockSpec(memory_space=pltpu.VMEM)] * 9,
+        in_specs=[pl.BlockSpec(memory_space=pltpu.VMEM)] * 6,
         out_specs=pl.BlockSpec(memory_space=pltpu.VMEM),
         scratch_shapes=[
             pltpu.VMEM((nh, 64, 256), f32),
@@ -168,7 +173,7 @@
             pltpu.VMEM((nh, 64, 128), f32),
         ],
         compiler_params=pltpu.CompilerParams(vmem_limit_bytes=48 * 1024 * 1024),
-    )(x, cos, sin, gain, shift, w1, c1, w2, c2)
+    )(x, cos, sin, gain, shift, own)
 
 
 def tables(off, n):
@@ -195,20 +200,14 @@
 ):
     groups = lax.axis_size("seq")
     nh, tok = first_weight.shape[1], query_proj.shape[1]
-    source = owner_map[lax.axis_index("branch")]
-
-    w2t = jnp.swapaxes(second_weight[0], 1, 2)
-    packed = jnp.concatenate([first_weight[0], w2t], 0).reshape(16, 24, 256)
+
+    weights = jnp.stack([first_weight[0], jnp.swapaxes(second_weight[0], 1, 2)])
+    weights = weights.reshape(2, nh, 8, 8, 256).transpose(0, 2, 3, 1, 4).reshape(16, 8, nh * 256)
+    biases = jnp.concatenate([first_bias[0, :, :128], first_bias[0, :, 128:], jnp.pad(second_bias[0].reshape(1, nh * 64), ((0, 0), (0, 64))).reshape(2, 128)], 0)
+    packed = jnp.concatenate([weights, jnp.broadcast_to(biases, (16, 8, 128))], 2)
     held = lax.all_to_all(packed, "branch", split_axis=0, concat_axis=0, tiled=True)
     picked = jnp.take(held, owner_map, axis=0)
     own = lax.all_to_all(picked, "branch", split_axis=0, concat_axis=0, tiled=True)
-    own = own.reshape(2 * nh, 64, 256)
-    biases = lax.all_gather(jnp.concatenate([first_bias[0], second_bias[0]], 1), "branch")
-    bias = lax.dynamic_index_in_dim(biases, source, 0, keepdims=False)
-    w1, w2 = own[:nh], own[nh:]
-    w2 = w2 - jnp.mean(w2, 1, keepdims=True)
-    c1, c2 = bias[:, :256], bias[:, 256:]
-    c2 = c2 - jnp.mean(c2, 1, keepdims=True)
 
     def column(x):
         return jnp.broadcast_to(x[:, :, None], x.shape + (128,))
@@ -220,7 +219,7 @@
     x = jnp.concatenate([by_group(query_proj), by_group(key_proj), by_group(value_proj), rates], 1)
     x = lax.all_to_all(x, "seq", split_axis=0, concat_axis=0, tiled=True)
     cos, sin = tables(start_offset[0], groups * tok)
-    y = ttt(x, cos, sin, column(norm_gain), column(norm_shift), w1, c1[:, None, :], w2, column(c2))
+    y = ttt(x, cos, sin, column(norm_gain), column(norm_shift), own)
     y = lax.all_to_all(y, "seq", split_axis=0, concat_axis=0, tiled=True)
     return y.reshape(groups * nh * 64, tok).T[None]
 

time: 240 us -> 208 us (0.87)
  blocking collectives: 114 us -> 24.7 us
  waiting for transfers between devices: 17.2 us -> 71.2 us
  local copies, waits for them, and re-layouts: 9.58 us -> 12.6 us
    all_gather x1 -> x0, blocking collectives: 79 us -> none  [body(): lax.all_gather(jnp.concatenate([first_bias[0], second_bias[0]], 1), 'bran...]
    all_to_all x1, waiting for transfers between devices: 0.01 us -> 54.1 us  [body(): x = lax.all_to_all(x, 'seq', split_axis=0, concat_axis=0, tiled=True)]
    all_to_all x1, blocking collectives: 34.8 us -> 24.7 us  [body(): y = lax.all_to_all(y, 'seq', split_axis=0, concat_axis=0, tiled=True)]
  transfers between devices with their start and end apart: 3 -> 3, of which waited for: 2 -> 3; matrix products, arithmetic and copies ran while one was open for 6% -> 7% of each run, Pallas kernels for 0% -> 0%
where the time goes in v2:
time: 208 us; the launch traced here: 207 us
  waiting for transfers between devices  71.2 us (34%)
  Pallas kernels  63.2 us (30%)
  starting transfers between devices  25.3 us (12%)
  blocking collectives  24.7 us (12%)
  local copies, waits for them, and re-layouts  12.6 us (6%)
  other arithmetic  9.46 us (5%)
    pallas_call x1, Pallas kernels, ttt(): pl.pallas_call(ttt_kernel, out_shape=jax.ShapeDtypeStruct((x.shape[0], nh...  63.2 us
    all_to_all x1, waiting for transfers between devices, body(): x = lax.all_to_all(x, 'seq', split_axis=0, concat_axis=0, tiled=True)  54.1 us
    all_to_all x1, blocking collectives, body(): y = lax.all_to_all(y, 'seq', split_axis=0, concat_axis=0, tiled=True)  24.7 us
    all_to_all x1, waiting for transfers between devices, body(): lax.all_to_all(packed, 'branch', split_axis=0, concat_axis=0, tiled=True)  14.1 us
    all_to_all x1, starting transfers between devices, body(): lax.all_to_all(packed, 'branch', split_axis=0, concat_axis=0, tiled=True)  11.6 us
    all_to_all x1, starting transfers between devices, body(): x = lax.all_to_all(x, 'seq', split_axis=0, concat_axis=0, tiled=True)  9.9 us
    transpose x3, local copies, waits for them, and re-layouts, by_group(): return x[0].T.reshape(groups, x.shape[2] // groups, tok)  6.89 us
  transfers between devices with their start and end apart: 3, of which 3 were waited for; matrix products, arithmetic and copies ran while one was open for 7% of the time, Pallas kernels for 0%

profile of v2, /device:TPU:1, one launch (start us, length us, event | category | flops | bytes accessed | tf_op | source)
XLA Modules:
  0.0 207.3 jit_solution(11431942560646570227)
XLA Ops:
  0.0 0.7 reduce
  0.8 0.7 fusion.2
  1.5 1.1 copy.22
  2.6 1.1 copy.21
  3.8 0.3 reshape.51
  4.1 0.8 pad_maximum_fusion
  4.9 11.6 %all-to-all-start.1 = ((f32[16,8,896]{2,1,0:T(8,128)}), f32[16,8,896]{2,1,0:T(8,128)S(1)}, u32[]{:S(2)}, u32[]{:S(2)}) async-start(f32[16,8,896]{2,1,0:T(8,128)} %pad_maximum_fusion), calls=%async_computation.1 | async-start | bytes 917504 | tf_op jit(solution)/shard_map/all_to_all | solution.py:208
  16.5 0.7 compare_select_fusion
  17.2 0.7 compare_and_fusion
  17.8 14.1 %all-to-all-done.1 = f32[16,8,896]{2,1,0:T(8,128)S(1)} async-done(((f32[16,8,896]{2,1,0:T(8,128)}), f32[16,8,896]{2,1,0:T(8,128)S(1)}, u32[]{:S(2)}, u32[]{:S(2)}) %all-to-all-start.1) | async-done | bytes 458784 | tf_op jit(solution)/shard_map/all_to_all | solution.py:208
  31.9 0.6 gather_fusion
  32.5 0.9 broadcast_select_fusion
  33.4 3.8 %all-to-all-start.2 = ((f32[16,8,896]{2,1,0:T(8,128)}), f32[16,8,896]{2,1,0:T(8,128)S(1)}, u32[]{:S(2)}, u32[]{:S(2)}) async-start(f32[16,8,896]{2,1,0:T(8,128)} %broadcast_select_fusion), calls=%async_computation.2 | async-start | bytes 917504 | tf_op jit(solution)/shard_map/all_to_all | solution.py:210
  37.2 1.7 copy.20
  38.9 2.6 %copy.19 = bf16[3072,256]{1,0:T(8,128)(2,1)} copy(bf16[3072,256]{0,1:T(8,128)(2,1)} %bitcast.39) | data formatting | bytes 3145728 | tf_op jit(solution)/shard_map/transpose | solution.py:216
  41.5 2.6 %copy.18 = bf16[3072,256]{1,0:T(8,128)(2,1)} copy(bf16[3072,256]{0,1:T(8,128)(2,1)} %bitcast.40) | data formatting | bytes 3145728 | tf_op jit(solution)/shard_map/transpose | solution.py:216
  44.1 3.7 %fusion.1 = bf16[16,592,256]{2,1,0:T(8,128)(2,1)} fusion(bf16[16,3,256]{2,1,0:T(4,128)(2,1)S(1)} %reshape.50, bf16[16,192,256]{2,1,0:T(8,128)(2,1)S(1)} %bitcast.34, bf16[16,192,256]{2,1,0:T(8,128)(2,1)} %bitcast.35, bf16[16,192,256]{2,1,0:T(8,128)(2,1)} %bitcast.36), kind=kLoop, calls=%fused_computation.3 | loop fusion | flops 24248320 | bytes 9592832 | tf_op jit(solution)/shard_map/concatenate | solution.py:219
  47.8 3.0 %all-to-all-done.2.own_ref = f32[16,8,896]{2,1,0:T(8,128)S(1)} async-done(((f32[16,8,896]{2,1,0:T(8,128)}), f32[16,8,896]{2,1,0:T(8,128)S(1)}, u32[]{:S(2)}, u32[]{:S(2)}) %all-to-all-start.2) | async-done | bytes 458784 | tf_op jit(solution)/shard_map/all_to_all | solution.py:210
  50.8 9.9 %all-to-all-start = ((bf16[16,592,256]{2,1,0:T(8,128)(2,1)}), bf16[16,592,256]{2,1,0:T(8,128)(2,1)}, u32[]{:S(2)}, u32[]{:S(2)}) async-start(bf16[16,592,256]{2,1,0:T(8,128)(2,1)} %fusion.1), calls=%async_computation | async-start | bytes 9699328 | tf_op jit(solution)/shard_map/all_to_all | solution.py:220
  61.4 1.9 multiply_sine_fusion
  63.3 54.1 %all-to-all-done.x_ref = bf16[16,592,256]{2,1,0:T(8,128)(2,1)} async-done(((bf16[16,592,256]{2,1,0:T(8,128)(2,1)}), bf16[16,592,256]{2,1,0:T(8,128)(2,1)}, u32[]{:S(2)}, u32[]{:S(2)}) %all-to-all-start) | async-done | bytes 4849696 | tf_op jit(solution)/shard_map/all_to_all | solution.py:220
  117.6 63.2 %shard_map.118 = bf16[16,192,256]{2,1,0:T(8,128)(2,1)S(1)} custom-call(bf16[16,592,256]{2,1,0:T(8,128)(2,1)} %all-to-all-done.x_ref, f32[16,32,256]{2,1,0:T(8,128)S(1)} %get-tuple-element.6.cos_ref, f32[16,32,256]{2,1,0:T(8,128)S(1)} %get-tuple-element.5.sin_ref, f32[3,64,128]{2,1,0:T(8,128)S(1)} %broadcast_in_dim.31.gain_ref, ...), custom_call_target="tpu_custom_call" | custom-call | tf_op jit(solution)/shard_map/pallas_call | solution.py:162
  180.8 24.7 %all_to_all.20 = bf16[16,192,256]{2,1,0:T(8,128)(2,1)S(1)} all-to-all(bf16[16,192,256]{2,1,0:T(8,128)(2,1)S(1)} %shard_map.118), channel_id=1, replica_groups=mesh['branch'=16,'seq'=16] {'seq'}, dimensions={0} | all-to-all | bytes 3145728 | tf_op jit(solution)/shard_map/all_to_all | solution.py:223
  205.5 1.7 copy.24
  (18 shorter events, 0.5 us)
Async XLA Ops:
  0.0 37.2 %copy-start = (bf16[1,256,48]{1,2,0:T(8,128)(2,1)S(1)}, bf16[1,256,48]{1,2,0:T(8,128)(2,1)}, u32[]{:S(2)}) copy-start(bf16[1,256,48]{1,2,0:T(8,128)(2,1)} %param.15) | copy-start | bytes 73732
  4.9 27.0 %all-to-all-start.1 = ((f32[16,8,896]{2,1,0:T(8,128)}), f32[16,8,896]{2,1,0:T(8,128)S(1)}, u32[]{:S(2)}, u32[]{:S(2)}) async-start(f32[16,8,896]{2,1,0:T(8,128)} %pad_maximum_fusion), calls=%async_computation.1 | async-start | bytes 917504 | tf_op jit(solution)/shard_map/all_to_all | solution.py:208
  33.4 17.5 %all-to-all-start.2 = ((f32[16,8,896]{2,1,0:T(8,128)}), f32[16,8,896]{2,1,0:T(8,128)S(1)}, u32[]{:S(2)}, u32[]{:S(2)}) async-start(f32[16,8,896]{2,1,0:T(8,128)} %broadcast_select_fusion), calls=%async_computation.2 | async-start | bytes 917504 | tf_op jit(solution)/shard_map/all_to_all | solution.py:210
  47.8 69.6 %copy-start.1 = (f32[3,64]{1,0:T(4,128)S(1)}, f32[3,64]{1,0:T(4,128)}, u32[]{:S(2)}) copy-start(f32[3,64]{1,0:T(4,128)} %param.16) | copy-start | bytes 2308
  47.8 69.7 %copy-start.2 = (f32[3,64]{1,0:T(4,128)S(1)}, f32[3,64]{1,0:T(4,128)}, u32[]{:S(2)}) copy-start(f32[3,64]{1,0:T(4,128)} %param.17) | copy-start | bytes 2308
  50.8 66.6 %all-to-all-start = ((bf16[16,592,256]{2,1,0:T(8,128)(2,1)}), bf16[16,592,256]{2,1,0:T(8,128)(2,1)}, u32[]{:S(2)}, u32[]{:S(2)}) async-start(bf16[16,592,256]{2,1,0:T(8,128)(2,1)} %fusion.1), calls=%async_computation | async-start | bytes 9699328 | tf_op jit(solution)/shard_map/all_to_all | solution.py:220

commit v3 on v2

v3 whole, which is shorter than its diff:
```python
import jax
import jax.numpy as jnp
from jax import lax
from jax.experimental import pallas as pl
from jax.experimental.pallas import tpu as pltpu
from jax.sharding import PartitionSpec as P

f32, bf16 = jnp.float32, jnp.bfloat16
C0 = 0.7978845608028654
C1 = 0.044715
MB = 64


def split(x):
    hi = x.astype(bf16)
    return hi, (x - hi.astype(f32)).astype(bf16)


def stack4(hi, lo, axis):
    return jnp.concatenate([hi, lo, hi, lo], axis)


def dot(a, b):
    return jnp.dot(a, b, preferred_element_type=f32)


def dot_nt(a, b):
    return lax.dot_general(a, b, (((1,), (1,)), ((), ())), preferred_element_type=f32)


def ttt_kernel(x_ref, cos_ref, sin_ref, gain_ref, shift_ref, own_ref, out_ref,
               w1_ref, c1_ref, w2_ref, c2_ref, yprev_ref, base_ref, corr_ref, dh_ref,
               xk_ref, xq_ref, xt_ref, xd_ref, rate_ref):
    nh = w1_ref.shape[0]
    heads = range(nh)
    nb = x_ref.shape[0]
    rows = nh * 64
    for h in heads:
        hl = slice(h * 256, h * 256 + 256)
        for i in range(8):
            w1_ref[h, i * 8:i * 8 + 8] = own_ref[i, :, hl]
        w2 = jnp.concatenate([own_ref[8 + i, :, hl] for i in range(8)], 0)
        w2_ref[h] = 0.5 * (w2 - jnp.mean(w2, 0, keepdims=True))
        bias = own_ref[0, :, nh * 256:nh * 256 + 128]
        c1_ref[h] = jnp.concatenate([bias[h:h + 1], bias[nh + h:nh + h + 1]], 1)
        c2 = bias[2 * nh + h // 2:2 * nh + h // 2 + 1, h % 2 * 64:h % 2 * 64 + 64]
        c2_ref[h] = jnp.transpose(jnp.broadcast_to(c2 - jnp.mean(c2), (128, 64)))
    yprev_ref[...] = jnp.zeros_like(yprev_ref)
    dh_ref[...] = jnp.zeros_like(dh_ref)
    corr_ref[...] = jnp.zeros_like(corr_ref)
    low = lax.broadcasted_iota(jnp.int32, (64, 128), 1) < 64
    low1 = lax.broadcasted_iota(jnp.int32, (1, 128), 1) < 64

    def tokmajor(x):
        return split(jnp.transpose(jnp.concatenate([x, x], 0)))

    def rot(x, cs, sn):
        a, b = x[:32], x[32:]
        return jnp.concatenate([a * cs - b * sn, a * sn + b * cs], 0)

    def prep(b, tile):
        ts = slice(tile * 128, tile * 128 + 128)
        cs, sn = cos_ref[b, :, ts], sin_ref[b, :, ts]
        rates = x_ref[b, 3 * rows:3 * rows + 16, ts].astype(f32) * (1.0 / MB)
        out = []
        for h in heads:
            q = rot(x_ref[b, h * 64:h * 64 + 64, ts].astype(f32), cs, sn)
            k = rot(x_ref[b, rows + h * 64:rows + h * 64 + 64, ts].astype(f32), cs, sn)
            v = x_ref[b, 2 * rows + h * 64:2 * rows + h * 64 + 64, ts].astype(f32)
            target = gain_ref[h] * (shift_ref[h] - (v - k))
            target = target - jnp.mean(target, 0, keepdims=True)
            kr = pltpu.roll(k, 64, 1)
            even = jnp.concatenate(split(jnp.where(low, k, kr)), 1)
            odd = jnp.concatenate(split(jnp.where(low, kr, k)), 1)
            out.append((k, q, target, even, odd, rates[h:h + 1]))
        return tuple(list(x) for x in zip(*out))

    def normed(z):
        c = z - jnp.mean(z, 0, keepdims=True)
        return c, lax.rsqrt(jnp.mean(c * c, 0, keepdims=True) + 1e-06)

    def hidden(xds):
        upd = [dot(jnp.concatenate([corr_ref[h], xds[h]], 0), stack4(dh_ref[h, :64], dh_ref[h, 64:], 0)) for h in heads]
        return [base_ref[h] - upd[h][:128] for h in heads], [u[128:] for u in upd]

    def gelu(hid, sl):
        act, slope = [], []
        for x in hid:
            sq = x * x
            th = jnp.tanh(x * (sq * (C0 * C1) + C0))
            act.append(split(x * th + x))
            if sl is not None:
                t, v = th[sl], x[sl]
                slope.append((1.0 + t) * ((v * (sq[sl] * (3 * C0 * C1) + C0)) * (1.0 - t) + 1.0))
        return act, slope

    def second(aa, ww):
        z4 = [dot_nt(jnp.concatenate(ww[h], 0), jnp.concatenate(aa[h], 0)) for h in heads]
        return [(z[:64, :128] + z[64:, 128:]) + (z[64:, :128] + z[:64, 128:]) + c2_ref[h] for h, z in enumerate(z4)]

    def ahead(xs, xds, w1, c1):
        for h in heads:
            base_ref[h] = dot(xs[h], stack4(*split(w1[h]), 0)) + c1[h]
        for h in heads:
            hi, lo = xds[h][:, :128], xds[h][:, 128:]
            corr_ref[h] = jnp.concatenate(split(dot(xs[h], stack4(hi, lo, 0)) + 1.0), 1)

    def step(pq, target, rate, xprev, xds, xnext, even):
        sl = slice(0, 64) if even else slice(64, 128)
        hid, dw1 = hidden(xprev)
        aa, gp = gelu(hid, sl)
        w1 = [w1_ref[h] - dw1[h] for h in heads]
        c1 = [c1_ref[h] for h in heads]
        ww = [split(w2_ref[h]) for h in heads]
        z = second(aa, ww)
        ahead([jnp.concatenate(tokmajor(x), 1) for x in xnext], xds, w1, c1)
        dz, y = [], []
        for h in heads:
            c, rstd = normed(z[h])
            gain = gain_ref[h]
            y.append(c * rstd * gain + pq[h])
            g2c = gain * gain * c
            m2 = jnp.mean(g2c, 0, keepdims=True)
            m3 = jnp.mean(g2c * c, 0, keepdims=True)
            m4 = jnp.mean(target[h] * c, 0, keepdims=True)
            s = rstd * rate[h]
            e = rstd * rstd * (rstd * m3 + m4)
            dz.append(s * ((g2c - m2) * rstd + target[h] - c * e))
        lhs = []
        for h in heads:
            dzh, dzl = tokmajor(dz[h])
            lhs.append(jnp.concatenate([dzh[sl], dzl[sl]], 1))
        da = [dot(lhs[h], stack4(*ww[h], 0)) for h in heads]
        dh = [da[h] * gp[h] for h in heads]
        for h in heads:
            dh_ref[h] = jnp.concatenate(split(dh[h]), 0)
        dw2 = []
        for h in heads:
            d = dz[h] + pltpu.roll(dz[h], 64, 1)
            dw2.append(dot(jnp.concatenate(split(d), 1), stack4(aa[h][0][sl], aa[h][1][sl], 0)))
        for h in heads:
            w2_ref[h] = w2_ref[h] - 0.25 * dw2[h]
            c2_ref[h] = c2_ref[h] - jnp.sum(dz[h], 1, keepdims=True)
            w1_ref[h] = w1[h]
            c1_ref[h] = c1[h] - jnp.sum(dh[h], 0, keepdims=True)
        return y

    def tile_steps(cur, nxt, qp, xp):
        k, q, target, even, odd, rate = cur
        ye = step([qp[h] + shift_ref[h] for h in heads], target, [jnp.where(low1, r, 0.0) for r in rate],
                  xp, even, [jnp.where(low, q[h], k[h]) for h in heads], True)
        yo = step([q[h] + shift_ref[h] for h in heads], target, [jnp.where(low1, 0.0, r) for r in rate],
                  even, odd, [jnp.where(low, nxt[0][h], q[h]) for h in heads], False)
        return ye, yo

    def put(b, tile, first, then):
        for h in heads:
            out_ref[b, h * 64:h * 64 + 64, tile * 128:tile * 128 + 128] = jnp.where(low, first[h], then[h]).astype(bf16)

    def save(cur, qp, xp):
        for h in heads:
            xk_ref[h], xq_ref[h], xt_ref[h] = cur[0][h], cur[1][h], cur[2][h]
            xd_ref[0, h], xd_ref[1, h], xd_ref[2, h] = cur[3][h], cur[4][h], xp[h]
            rate_ref[h], xq_ref[nh + h] = cur[5][h], qp[h]

    def block(b, _):
        cur = ([xk_ref[h] for h in heads], [xq_ref[h] for h in heads], [xt_ref[h] for h in heads],
               [xd_ref[0, h] for h in heads], [xd_ref[1, h] for h in heads], [rate_ref[h] for h in heads])
        mid = prep(b, 1)
        ye, yo = tile_steps(cur, mid, [xq_ref[nh + h] for h in heads], [xd_ref[2, h] for h in heads])
        put(jnp.maximum(b - 1, 0), 1, [yprev_ref[h] for h in heads], ye)
        end = prep(jnp.minimum(b + 1, nb - 1), 0)
        ye, yn = tile_steps(mid, end, cur[1], cur[4])
        put(b, 0, yo, ye)
        for h in heads:
            yprev_ref[h] = yn[h]
        save(end, mid[1], mid[4])
        return 0

    first = prep(0, 0)
    zero = [jnp.zeros((64, 128), f32) for h in heads]
    none = [jnp.zeros((64, 256), bf16) for h in heads]
    for h in heads:
        xs = jnp.concatenate(tokmajor(first[0][h]), 1)
        base_ref[h] = dot(xs, stack4(*split(w1_ref[h]), 0)) + c1_ref[h]
    save(first, zero, none)
    lax.fori_loop(0, nb, block, 0)
    hid, _ = hidden([xd_ref[2, h] for h in heads])
    z = second(gelu(hid, None)[0], [split(w2_ref[h]) for h in heads])
    last = []
    for h in heads:
        c, rstd = normed(z[h])
        last.append(c * rstd * gain_ref[h] + xq_ref[nh + h] + shift_ref[h])
    put(nb - 1, 1, [yprev_ref[h] for h in heads], last)


def ttt(x, cos, sin, gain, shift, own):
    nh = gain.shape[0]
    return pl.pallas_call(
        ttt_kernel,
        out_shape=jax.ShapeDtypeStruct((x.shape[0], nh * 64, x.shape[2]), bf16),
        in_specs=[pl.BlockSpec(memory_space=pltpu.VMEM)] * 6,
        out_specs=pl.BlockSpec(memory_space=pltpu.VMEM),
        scratch_shapes=[
            pltpu.VMEM((nh, 64, 256), f32),
            pltpu.VMEM((nh, 1, 256), f32),
            pltpu.VMEM((nh, 64, 256), f32),
            pltpu.VMEM((nh, 64, 128), f32),
            pltpu.VMEM((nh, 64, 128), f32),
            pltpu.VMEM((nh, 128, 256), f32),
            pltpu.VMEM((nh, 128, 256), bf16),
            pltpu.VMEM((nh, 128, 256), bf16),
            pltpu.VMEM((nh, 64, 128), f32),
            pltpu.VMEM((2 * nh, 64, 128), f32),
            pltpu.VMEM((nh, 64, 128), f32),
            pltpu.VMEM((3, nh, 64, 256), bf16),
            pltpu.VMEM((nh, 1, 128), f32),
        ],
        compiler_params=pltpu.CompilerParams(vmem_limit_bytes=48 * 1024 * 1024),
    )(x, cos, sin, gain, shift, own)


def pack_kernel(w1_ref, c1_ref, w2_ref, c2_ref, out_ref):
    nh = w1_ref.shape[0]
    c1, c2 = c1_ref[...], c2_ref[...]
    for h in range(nh):
        hl = slice(h * 256, h * 256 + 256)
        w2 = jnp.transpose(w2_ref[h])
        for i in range(8):
            out_ref[i, :, hl] = w1_ref[h, i * 8:i * 8 + 8]
            out_ref[8 + i, :, hl] = w2[i * 8:i * 8 + 8]
    out_ref[:, :, nh * 256:] = jnp.zeros_like(out_ref[:, :, nh * 256:])
    for i in range(16):
        out_ref[i, :nh, nh * 256:] = c1[:, :128]
        out_ref[i, nh:2 * nh, nh * 256:] = c1[:, 128:]
        for h in range(nh):
            at = nh * 256 + h % 2 * 64
            out_ref[i, 2 * nh + h // 2:2 * nh + h // 2 + 1, at:at + 64] = c2[h:h + 1]


def pack(w1, c1, w2, c2):
    return pl.pallas_call(
        pack_kernel,
        out_shape=jax.ShapeDtypeStruct((16, 8, w1.shape[0] * 256 + 128), f32),
        in_specs=[pl.BlockSpec(memory_space=pltpu.VMEM)] * 4,
        out_specs=pl.BlockSpec(memory_space=pltpu.VMEM),
        compiler_params=pltpu.CompilerParams(vmem_limit_bytes=16 * 1024 * 1024),
    )(w1, c1, w2, c2)


def tables(off, n):
    half = 32
    freqs = jnp.exp(-jnp.log(10000.0) * jnp.arange(half, dtype=f32) / half)
    pos = (off + jnp.arange(n, dtype=jnp.int32)).astype(f32)
    ang = pos.reshape(n // 256, 1, 256) * freqs[None, :, None]
    return jnp.cos(ang), jnp.sin(ang)


def body(
    query_proj,
    key_proj,
    value_proj,
    learn_rate,
    norm_gain,
    norm_shift,
    start_offset,
    owner_map,
    first_weight,
    first_bias,
    second_weight,
    second_bias,
):
    groups = lax.axis_size("seq")
    nh, tok = first_weight.shape[1], query_proj.shape[1]

    packed = pack(first_weight[0], first_bias[0], second_weight[0], second_bias[0])
    held = lax.all_to_all(packed, "branch", split_axis=0, concat_axis=0, tiled=True)
    picked = held.at[owner_map].get(mode="promise_in_bounds")
    own = lax.all_to_all(picked, "branch", split_axis=0, concat_axis=0, tiled=True)

    def column(x):
        return jnp.broadcast_to(x[:, :, None], x.shape + (128,))

    def by_group(x):
        return x[0].T.reshape(groups, x.shape[2] // groups, tok)

    rates = jnp.pad(by_group(learn_rate), ((0, 0), (0, 16 - nh), (0, 0)))
    x = jnp.concatenate([by_group(query_proj), by_group(key_proj), by_group(value_proj), rates], 1)
    x = lax.all_to_all(x, "seq", split_axis=0, concat_axis=0, tiled=True)
    cos, sin = tables(start_offset[0], groups * tok)
    y = ttt(x, cos, sin, column(norm_gain), column(norm_shift), own)
    y = lax.all_to_all(y, "seq", split_axis=0, concat_axis=0, tiled=True)
    return y.reshape(groups * nh * 64, tok).T[None]


def solution(mesh):
    return jax.shard_map(
        body,
        mesh=mesh,
        in_specs=(
            P("branch", "seq", None),
            P("branch", "seq", None),
            P("branch", "seq", None),
            P("branch", "seq", None),
            P("seq", None),
            P("seq", None),
            P("branch"),
            P(),
            P("branch", "seq", None, None),
            P("branch", "seq", None),
            P("branch", "seq", None, None),
            P("branch", "seq", None),
        ),
        out_specs=P("branch", "seq", None),
        check_vma=False,
    )
```

time: 208 us -> 198 us (0.952)
  Pallas kernels: 63.2 us -> 54.8 us
  other arithmetic: 9.46 us -> 6.27 us
    pallas_call x1, Pallas kernels: 63.2 us -> 53.9 us  [ttt(): pl.pallas_call(ttt_kernel, out_shape=jax.ShapeDtypeStruct((x.shape[0], nh...]
    unnamed x6 -> x9, local copies, waits for them, and re-layouts: 0.01 us -> 3.39 us
    another operation x3 -> x0, local copies, waits for them, and re-layouts: 2.21 us -> none  [the longest x2 2.13 us: body(): weights = jnp.stack([first_weight[0], jnp.swapaxes(second_weight[0], 1, 2)])]
where the time goes in v3:
time: 198 us; the launch traced here: 197 us
  waiting for transfers between devices  71.2 us (36%)
  Pallas kernels  54.8 us (28%)
  starting transfers between devices  25.3 us (13%)
  blocking collectives  24.7 us (12%)
  local copies, waits for them, and re-layouts  14.3 us (7%)
  other arithmetic  6.27 us (3%)
    all_to_all x1, waiting for transfers between devices, body(): x = lax.all_to_all(x, 'seq', split_axis=0, concat_axis=0, tiled=True)  54.1 us
    pallas_call x1, Pallas kernels, ttt(): pl.pallas_call(ttt_kernel, out_shape=jax.ShapeDtypeStruct((x.shape[0], nh...  53.9 us
    all_to_all x1, blocking collectives, body(): y = lax.all_to_all(y, 'seq', split_axis=0, concat_axis=0, tiled=True)  24.7 us
    all_to_all x1, waiting for transfers between devices, body(): lax.all_to_all(packed, 'branch', split_axis=0, concat_axis=0, tiled=True)  14.7 us
    all_to_all x1, starting transfers between devices, body(): lax.all_to_all(packed, 'branch', split_axis=0, concat_axis=0, tiled=True)  11.6 us
    all_to_all x1, starting transfers between devices, body(): x = lax.all_to_all(x, 'seq', split_axis=0, concat_axis=0, tiled=True)  9.9 us
    transpose x3, local copies, waits for them, and re-layouts, by_group(): return x[0].T.reshape(groups, x.shape[2] // groups, tok)  6.89 us
  transfers between devices with their start and end apart: 3, of which 3 were waited for; matrix products, arithmetic and copies ran while one was open for 7% of the time, Pallas kernels for 0%

profile of v3, /device:TPU:1, one launch (start us, length us, event | category | flops | bytes accessed | tf_op | source)
XLA Modules:
  0.0 197.2 jit_solution(7133858106632235268)
XLA Ops:
  0.0 0.7 copy.27
  0.7 1.1 copy.21
  1.8 0.7 copy.28
  2.5 0.9 copy-done
  3.4 0.9 shard_map.118
  4.3 11.6 %all-to-all-start.1 = ((f32[16,8,896]{2,1,0:T(8,128)}), f32[16,8,896]{2,1,0:T(8,128)S(1)}, u32[]{:S(2)}, u32[]{:S(2)}) async-start(f32[16,8,896]{2,1,0:T(8,128)} %shard_map.118), calls=%async_computation.1 | async-start | bytes 917504 | tf_op jit(solution)/shard_map/all_to_all | solution.py:277
  15.9 0.7 compare_select_fusion
  16.6 14.7 %all-to-all-done.1 = f32[16,8,896]{2,1,0:T(8,128)S(1)} async-done(((f32[16,8,896]{2,1,0:T(8,128)}), f32[16,8,896]{2,1,0:T(8,128)S(1)}, u32[]{:S(2)}, u32[]{:S(2)}) %all-to-all-start.1) | async-done | bytes 458784 | tf_op jit(solution)/shard_map/all_to_all | solution.py:277
  31.3 1.4 gather_fusion
  32.7 3.8 %all-to-all-start.2 = ((f32[16,8,896]{2,1,0:T(8,128)}), f32[16,8,896]{2,1,0:T(8,128)S(1)}, u32[]{:S(2)}, u32[]{:S(2)}) async-start(f32[16,8,896]{2,1,0:T(8,128)} %gather_fusion), calls=%async_computation.2 | async-start | bytes 917504 | tf_op jit(solution)/shard_map/all_to_all | solution.py:279
  36.5 0.8 reshape.35
  37.3 1.7 copy.20
  39.0 2.6 %copy.19 = bf16[3072,256]{1,0:T(8,128)(2,1)} copy(bf16[3072,256]{0,1:T(8,128)(2,1)} %bitcast.38) | data formatting | bytes 3145728 | tf_op jit(solution)/shard_map/transpose | solution.py:285
  41.5 2.6 %copy.18 = bf16[3072,256]{1,0:T(8,128)(2,1)} copy(bf16[3072,256]{0,1:T(8,128)(2,1)} %bitcast.39) | data formatting | bytes 3145728 | tf_op jit(solution)/shard_map/transpose | solution.py:285
  44.2 3.7 %fusion.1 = bf16[16,592,256]{2,1,0:T(8,128)(2,1)} fusion(bf16[16,3,256]{2,1,0:T(4,128)(2,1)S(1)} %reshape.35, bf16[16,192,256]{2,1,0:T(8,128)(2,1)S(1)} %bitcast.33, bf16[16,192,256]{2,1,0:T(8,128)(2,1)} %bitcast.34, bf16[16,192,256]{2,1,0:T(8,128)(2,1)} %bitcast.35), kind=kLoop, calls=%fused_computation.3 | loop fusion | flops 24248320 | bytes 9592832 | tf_op jit(solution)/shard_map/concatenate | solution.py:288
  47.9 2.3 %all-to-all-done.2.own_ref = f32[16,8,896]{2,1,0:T(8,128)S(1)} async-done(((f32[16,8,896]{2,1,0:T(8,128)}), f32[16,8,896]{2,1,0:T(8,128)S(1)}, u32[]{:S(2)}, u32[]{:S(2)}) %all-to-all-start.2) | async-done | bytes 458784 | tf_op jit(solution)/shard_map/all_to_all | solution.py:279
  50.1 9.9 %all-to-all-start = ((bf16[16,592,256]{2,1,0:T(8,128)(2,1)}), bf16[16,592,256]{2,1,0:T(8,128)(2,1)}, u32[]{:S(2)}, u32[]{:S(2)}) async-start(bf16[16,592,256]{2,1,0:T(8,128)(2,1)} %fusion.1), calls=%async_computation | async-start | bytes 9699328 | tf_op jit(solution)/shard_map/all_to_all | solution.py:289
  60.7 1.9 multiply_sine_fusion
  62.6 54.1 %all-to-all-done.x_ref = bf16[16,592,256]{2,1,0:T(8,128)(2,1)} async-done(((bf16[16,592,256]{2,1,0:T(8,128)(2,1)}), bf16[16,592,256]{2,1,0:T(8,128)(2,1)}, u32[]{:S(2)}, u32[]{:S(2)}) %all-to-all-start) | async-done | bytes 4849696 | tf_op jit(solution)/shard_map/all_to_all | solution.py:289
  116.8 0.1 broadcast_in_dim.8.gain_ref
  116.9 0.1 broadcast_in_dim.9.shift_ref
  116.9 53.9 %shard_map.119 = bf16[16,192,256]{2,1,0:T(8,128)(2,1)S(1)} custom-call(bf16[16,592,256]{2,1,0:T(8,128)(2,1)} %all-to-all-done.x_ref, f32[16,32,256]{2,1,0:T(8,128)S(1)} %get-tuple-element.6.cos_ref, f32[16,32,256]{2,1,0:T(8,128)S(1)} %get-tuple-element.5.sin_ref, f32[3,64,128]{2,1,0:T(8,128)S(1)} %broadcast_in_dim.8.gain_ref, ...), custom_call_target="tpu_custom_call" | custom-call | tf_op jit(solution)/shard_map/pallas_call | solution.py:199
  170.8 24.7 %all_to_all.20 = bf16[16,192,256]{2,1,0:T(8,128)(2,1)S(1)} all-to-all(bf16[16,192,256]{2,1,0:T(8,128)(2,1)S(1)} %shard_map.119), channel_id=1, replica_groups=mesh['branch'=16,'seq'=16] {'seq'}, dimensions={0} | all-to-all | bytes 3145728 | tf_op jit(solution)/shard_map/all_to_all | solution.py:292
  195.5 1.7 copy.22
  (8 shorter events, 0.0 us)
Async XLA Ops:
  2.5 0.9 copy-start
  4.3 27.0 %all-to-all-start.1 = ((f32[16,8,896]{2,1,0:T(8,128)}), f32[16,8,896]{2,1,0:T(8,128)S(1)}, u32[]{:S(2)}, u32[]{:S(2)}) async-start(f32[16,8,896]{2,1,0:T(8,128)} %shard_map.118), calls=%async_computation.1 | async-start | bytes 917504 | tf_op jit(solution)/shard_map/all_to_all | solution.py:277
  32.7 17.5 %all-to-all-start.2 = ((f32[16,8,896]{2,1,0:T(8,128)}), f32[16,8,896]{2,1,0:T(8,128)S(1)}, u32[]{:S(2)}, u32[]{:S(2)}) async-start(f32[16,8,896]{2,1,0:T(8,128)} %gather_fusion), calls=%async_computation.2 | async-start | bytes 917504 | tf_op jit(solution)/shard_map/all_to_all | solution.py:279
  47.8 68.9 %copy-start.1 = (f32[3,64]{1,0:T(4,128)S(1)}, f32[3,64]{1,0:T(4,128)}, u32[]{:S(2)}) copy-start(f32[3,64]{1,0:T(4,128)} %param.16) | copy-start | bytes 2308
  47.9 69.0 %copy-start.2 = (f32[3,64]{1,0:T(4,128)S(1)}, f32[3,64]{1,0:T(4,128)}, u32[]{:S(2)}) copy-start(f32[3,64]{1,0:T(4,128)} %param.17) | copy-start | bytes 2308
  50.1 66.6 %all-to-all-start = ((bf16[16,592,256]{2,1,0:T(8,128)(2,1)}), bf16[16,592,256]{2,1,0:T(8,128)(2,1)}, u32[]{:S(2)}, u32[]{:S(2)}) async-start(bf16[16,592,256]{2,1,0:T(8,128)(2,1)} %fusion.1), calls=%async_computation | async-start | bytes 9699328 | tf_op jit(solution)/shard_map/all_to_all | solution.py:289

commit v4 on v3

--- a/solution.py
+++ b/solution.py
@@ -9,6 +9,10 @@
 C0 = 0.7978845608028654
 C1 = 0.044715
 MB = 64
+UNROLL = 2
+SKEW = 2.0
+ORDER = (("prep", 0), ("upd", 1), ("gelu", 2), ("w2", 3), ("z", 4), ("w1", 5), ("x", 6), ("base", 7), ("corr", 8),
+         ("ln", 9), ("t", 10), ("da", 11), ("dh", 12), ("dw2", 13), ("state", 14), ("y", 15))
 
 
 def split(x):
@@ -58,140 +62,174 @@
         a, b = x[:32], x[32:]
         return jnp.concatenate([a * cs - b * sn, a * sn + b * cs], 0)
 
-    def prep(b, tile):
+    def prep(b, tile, h):
         ts = slice(tile * 128, tile * 128 + 128)
         cs, sn = cos_ref[b, :, ts], sin_ref[b, :, ts]
         rates = x_ref[b, 3 * rows:3 * rows + 16, ts].astype(f32) * (1.0 / MB)
-        out = []
-        for h in heads:
-            q = rot(x_ref[b, h * 64:h * 64 + 64, ts].astype(f32), cs, sn)
-            k = rot(x_ref[b, rows + h * 64:rows + h * 64 + 64, ts].astype(f32), cs, sn)
-            v = x_ref[b, 2 * rows + h * 64:2 * rows + h * 64 + 64, ts].astype(f32)
-            target = gain_ref[h] * (shift_ref[h] - (v - k))
-            target = target - jnp.mean(target, 0, keepdims=True)
-            kr = pltpu.roll(k, 64, 1)
-            even = jnp.concatenate(split(jnp.where(low, k, kr)), 1)
-            odd = jnp.concatenate(split(jnp.where(low, kr, k)), 1)
-            out.append((k, q, target, even, odd, rates[h:h + 1]))
-        return tuple(list(x) for x in zip(*out))
+        q = rot(x_ref[b, h * 64:h * 64 + 64, ts].astype(f32), cs, sn)
+        k = rot(x_ref[b, rows + h * 64:rows + h * 64 + 64, ts].astype(f32), cs, sn)
+        v = x_ref[b, 2 * rows + h * 64:2 * rows + h * 64 + 64, ts].astype(f32)
+        target = gain_ref[h] * (shift_ref[h] - (v - k))
+        target = target - jnp.mean(target, 0, keepdims=True)
+        kr = pltpu.roll(k, 64, 1)
+        even = split(jnp.where(low, k, kr))
+        odd = split(jnp.where(low, kr, k))
+        return k, q, target, jnp.concatenate(even, 1), jnp.concatenate(odd, 1), rates[h:h + 1]
+
+    refs = dict(w1=w1_ref, c1=c1_ref, w2=w2_ref, c2=c2_ref, base=base_ref, corr=corr_ref, dh=dh_ref)
+    live = {}
+
+    def load():
+        for name, ref in refs.items():
+            live[name] = [ref[h] for h in heads]
+
+    def store():
+        for name, ref in refs.items():
+            for h in heads:
+                ref[h] = live[name][h]
 
     def normed(z):
         c = z - jnp.mean(z, 0, keepdims=True)
         return c, lax.rsqrt(jnp.mean(c * c, 0, keepdims=True) + 1e-06)
 
-    def hidden(xds):
-        upd = [dot(jnp.concatenate([corr_ref[h], xds[h]], 0), stack4(dh_ref[h, :64], dh_ref[h, 64:], 0)) for h in heads]
-        return [base_ref[h] - upd[h][:128] for h in heads], [u[128:] for u in upd]
-
-    def gelu(hid, sl):
-        act, slope = [], []
-        for x in hid:
-            sq = x * x
-            th = jnp.tanh(x * (sq * (C0 * C1) + C0))
-            act.append(split(x * th + x))
-            if sl is not None:
-                t, v = th[sl], x[sl]
-                slope.append((1.0 + t) * ((v * (sq[sl] * (3 * C0 * C1) + C0)) * (1.0 - t) + 1.0))
-        return act, slope
-
-    def second(aa, ww):
-        z4 = [dot_nt(jnp.concatenate(ww[h], 0), jnp.concatenate(aa[h], 0)) for h in heads]
-        return [(z[:64, :128] + z[64:, 128:]) + (z[64:, :128] + z[:64, 128:]) + c2_ref[h] for h, z in enumerate(z4)]
-
-    def ahead(xs, xds, w1, c1):
-        for h in heads:
-            base_ref[h] = dot(xs[h], stack4(*split(w1[h]), 0)) + c1[h]
-        for h in heads:
-            hi, lo = xds[h][:, :128], xds[h][:, 128:]
-            corr_ref[h] = jnp.concatenate(split(dot(xs[h], stack4(hi, lo, 0)) + 1.0), 1)
-
-    def step(pq, target, rate, xprev, xds, xnext, even):
+    def hidden(h, xd):
+        dh = live["dh"][h]
+        upd = dot(jnp.concatenate([live["corr"][h], xd], 0), stack4(dh[:64], dh[64:], 0))
+        return live["base"][h] - upd[:128], upd[128:]
+
+    def gelu(x, sl):
+        sq = x * x
+        th = jnp.tanh(x * (sq * (C0 * C1) + C0))
+        act = split(x * th + x)
+        if sl is None:
+            return act, None
+        t, v = th[sl], x[sl]
+        return act, (1.0 + t) * ((v * (sq[sl] * (3 * C0 * C1) + C0)) * (1.0 - t) + 1.0)
+
+    def second(h, act, w2):
+        z = dot_nt(jnp.concatenate(w2, 0), jnp.concatenate(act, 0))
+        return (z[:64, :128] + z[64:, 128:]) + (z[64:, :128] + z[:64, 128:]) + live["c2"][h]
+
+    def step(b, tile, even, cur, last, nxt):
         sl = slice(0, 64) if even else slice(64, 128)
-        hid, dw1 = hidden(xprev)
-        aa, gp = gelu(hid, sl)
-        w1 = [w1_ref[h] - dw1[h] for h in heads]
-        c1 = [c1_ref[h] for h in heads]
-        ww = [split(w2_ref[h]) for h in heads]
-        z = second(aa, ww)
-        ahead([jnp.concatenate(tokmajor(x), 1) for x in xnext], xds, w1, c1)
-        dz, y = [], []
-        for h in heads:
-            c, rstd = normed(z[h])
-            gain = gain_ref[h]
-            y.append(c * rstd * gain + pq[h])
+        vs = [{} for h in heads]
+
+        def s_upd(h, v):
+            k, q, target, xe, xo, rate = cur[h]
+            v["hid"], v["dw1"] = hidden(h, last[h][4] if even else xe)
+
+        def s_gelu(h, v):
+            v["act"], v["slope"] = gelu(v["hid"], sl)
+
+        def s_w2(h, v):
+            v["w2"] = split(live["w2"][h])
+
+        def s_z(h, v):
+            v["z"] = second(h, v["act"], v["w2"])
+
+        def s_w1(h, v):
+            v["w1"] = live["w1"][h] - v["dw1"]
+            v["c1"] = live["c1"][h]
+
+        def s_x(h, v):
+            x = jnp.where(low, cur[h][1], cur[h][0]) if even else jnp.where(low, nxt[h][0], cur[h][1])
+            v["x"] = jnp.concatenate(tokmajor(x), 1)
+
+        def s_base(h, v):
+            live["base"][h] = dot(v["x"], stack4(*split(v["w1"]), 0)) + v["c1"]
+
+        def s_corr(h, v):
+            xd = cur[h][3 if even else 4]
+            live["corr"][h] = jnp.concatenate(split(dot(v["x"], stack4(xd[:, :128], xd[:, 128:], 0)) + 1.0), 1)
+
+        def s_ln(h, v):
+            c, rstd = normed(v["z"])
+            gain, target = gain_ref[h], cur[h][2]
+            rate = jnp.where(low1, cur[h][5], 0.0) if even else jnp.where(low1, 0.0, cur[h][5])
+            v["c"], v["rstd"] = c, rstd
             g2c = gain * gain * c
             m2 = jnp.mean(g2c, 0, keepdims=True)
             m3 = jnp.mean(g2c * c, 0, keepdims=True)
-            m4 = jnp.mean(target[h] * c, 0, keepdims=True)
-            s = rstd * rate[h]
+            m4 = jnp.mean(target * c, 0, keepdims=True)
             e = rstd * rstd * (rstd * m3 + m4)
-            dz.append(s * ((g2c - m2) * rstd + target[h] - c * e))
-        lhs = []
-        for h in heads:
-            dzh, dzl = tokmajor(dz[h])
-            lhs.append(jnp.concatenate([dzh[sl], dzl[sl]], 1))
-        da = [dot(lhs[h], stack4(*ww[h], 0)) for h in heads]
-        dh = [da[h] * gp[h] for h in heads]
-        for h in heads:
-            dh_ref[h] = jnp.concatenate(split(dh[h]), 0)
-        dw2 = []
-        for h in heads:
-            d = dz[h] + pltpu.roll(dz[h], 64, 1)
-            dw2.append(dot(jnp.concatenate(split(d), 1), stack4(aa[h][0][sl], aa[h][1][sl], 0)))
-        for h in heads:
-            w2_ref[h] = w2_ref[h] - 0.25 * dw2[h]
-            c2_ref[h] = c2_ref[h] - jnp.sum(dz[h], 1, keepdims=True)
-            w1_ref[h] = w1[h]
-            c1_ref[h] = c1[h] - jnp.sum(dh[h], 0, keepdims=True)
-        return y
-
-    def tile_steps(cur, nxt, qp, xp):
-        k, q, target, even, odd, rate = cur
-        ye = step([qp[h] + shift_ref[h] for h in heads], target, [jnp.where(low1, r, 0.0) for r in rate],
-                  xp, even, [jnp.where(low, q[h], k[h]) for h in heads], True)
-        yo = step([q[h] + shift_ref[h] for h in heads], target, [jnp.where(low1, 0.0, r) for r in rate],
-                  even, odd, [jnp.where(low, nxt[0][h], q[h]) for h in heads], False)
-        return ye, yo
+            v["dz"] = rstd * rate * ((g2c - m2) * rstd + target - c * e)
+
+        def s_t(h, v):
+            hi, lo = tokmajor(v["dz"])
+            v["dzt"] = jnp.concatenate([hi[sl], lo[sl]], 1)
+
+        def s_da(h, v):
+            v["da"] = dot(v["dzt"], stack4(*v["w2"], 0))
+
+        def s_dh(h, v):
+            v["dh"] = v["da"] * v["slope"]
+            live["dh"][h] = jnp.concatenate(split(v["dh"]), 0)
+
+        def s_dw2(h, v):
+            d = v["dz"] + pltpu.roll(v["dz"], 64, 1)
+            dw2 = dot(jnp.concatenate(split(d), 1), stack4(v["act"][0][sl], v["act"][1][sl], 0))
+            live["w2"][h] = live["w2"][h] - 0.25 * dw2
+            live["c2"][h] = live["c2"][h] - jnp.sum(v["dz"], 1, keepdims=True)
+
+        def s_state(h, v):
+            live["w1"][h] = v["w1"]
+            live["c1"][h] = v["c1"] - jnp.sum(v["dh"], 0, keepdims=True)
+
+        def s_y(h, v):
+            q = last[h][1] if even else cur[h][1]
+            v["y"] = v["c"] * v["rstd"] * gain_ref[h] + (q + shift_ref[h])
+
+        def s_prep(h, v):
+            if even:
+                nxt[h] = prep(b, tile, h)
+
+        stages = dict(upd=s_upd, gelu=s_gelu, w2=s_w2, z=s_z, w1=s_w1, x=s_x, base=s_base, corr=s_corr, ln=s_ln,
+                      t=s_t, da=s_da, dh=s_dh, dw2=s_dw2, state=s_state, y=s_y, prep=s_prep)
+        order = sorted((at + SKEW * h, i, h, name) for i, (name, at) in enumerate(ORDER) for h in heads)
+        for _, _, h, name in order:
+            stages[name](h, vs[h])
+        return [v["y"] for v in vs]
 
     def put(b, tile, first, then):
         for h in heads:
             out_ref[b, h * 64:h * 64 + 64, tile * 128:tile * 128 + 128] = jnp.where(low, first[h], then[h]).astype(bf16)
 
-    def save(cur, qp, xp):
+    def save(cur, last):
         for h in heads:
-            xk_ref[h], xq_ref[h], xt_ref[h] = cur[0][h], cur[1][h], cur[2][h]
-            xd_ref[0, h], xd_ref[1, h], xd_ref[2, h] = cur[3][h], cur[4][h], xp[h]
-            rate_ref[h], xq_ref[nh + h] = cur[5][h], qp[h]
+            xk_ref[h], xq_ref[h], xt_ref[h] = cur[h][0], cur[h][1], cur[h][2]
+            xd_ref[0, h], xd_ref[1, h], xd_ref[2, h] = cur[h][3], cur[h][4], last[h][4]
+            rate_ref[h], xq_ref[nh + h] = cur[h][5], last[h][1]
 
     def block(b, _):
-        cur = ([xk_ref[h] for h in heads], [xq_ref[h] for h in heads], [xt_ref[h] for h in heads],
-               [xd_ref[0, h] for h in heads], [xd_ref[1, h] for h in heads], [rate_ref[h] for h in heads])
-        mid = prep(b, 1)
-        ye, yo = tile_steps(cur, mid, [xq_ref[nh + h] for h in heads], [xd_ref[2, h] for h in heads])
-        put(jnp.maximum(b - 1, 0), 1, [yprev_ref[h] for h in heads], ye)
-        end = prep(jnp.minimum(b + 1, nb - 1), 0)
-        ye, yn = tile_steps(mid, end, cur[1], cur[4])
-        put(b, 0, yo, ye)
+        load()
+        cur = [(xk_ref[h], xq_ref[h], xt_ref[h], xd_ref[0, h], xd_ref[1, h], rate_ref[h]) for h in heads]
+        last = [(None, xq_ref[nh + h], None, None, xd_ref[2, h], None) for h in heads]
+        mid, end = [None] * nh, [None] * nh
+        y = step(b, 1, True, cur, last, mid)
+        put(jnp.maximum(b - 1, 0), 1, [yprev_ref[h] for h in heads], y)
+        first = step(b, 1, False, cur, last, mid)
+        then = step(jnp.minimum(b + 1, nb - 1), 0, True, mid, cur, end)
+        put(b, 0, first, then)
+        y = step(b, 0, False, mid, cur, end)
         for h in heads:
-            yprev_ref[h] = yn[h]
-        save(end, mid[1], mid[4])
+            yprev_ref[h] = y[h]
+        save(end, mid)
+        store()
         return 0
 
-    first = prep(0, 0)
-    zero = [jnp.zeros((64, 128), f32) for h in heads]
-    none = [jnp.zeros((64, 256), bf16) for h in heads]
+    first = [prep(0, 0, h) for h in heads]
     for h in heads:
-        xs = jnp.concatenate(tokmajor(first[0][h]), 1)
+        xs = jnp.concatenate(tokmajor(first[h][0]), 1)
         base_ref[h] = dot(xs, stack4(*split(w1_ref[h]), 0)) + c1_ref[h]
-    save(first, zero, none)
-    lax.fori_loop(0, nb, block, 0)
-    hid, _ = hidden([xd_ref[2, h] for h in heads])
-    z = second(gelu(hid, None)[0], [split(w2_ref[h]) for h in heads])
-    last = []
+    save(first, [(None, jnp.zeros((64, 128), f32), None, None, jnp.zeros((64, 256), bf16), None)] * nh)
+    lax.fori_loop(0, nb, block, 0, unroll=UNROLL)
+    load()
+    y = []
     for h in heads:
-        c, rstd = normed(z[h])
-        last.append(c * rstd * gain_ref[h] + xq_ref[nh + h] + shift_ref[h])
-    put(nb - 1, 1, [yprev_ref[h] for h in heads], last)
+        hid, _ = hidden(h, xd_ref[2, h])
+        c, rstd = normed(second(h, gelu(hid, None)[0], split(live["w2"][h])))
+        y.append(c * rstd * gain_ref[h] + (xq_ref[nh + h] + shift_ref[h]))
+    put(nb - 1, 1, [yprev_ref[h] for h in heads], y)
 
 
 def ttt(x, cos, sin, gain, shift, own):

time: 198 us -> 195 us (0.985)
  Pallas kernels: 54.8 us -> 52.2 us
    pallas_call x1, Pallas kernels: 53.9 us -> 51.2 us  [ttt(): pl.pallas_call(ttt_kernel, out_shape=jax.ShapeDtypeStruct((x.shape[0], nh...]
where the time goes in v4:
time: 195 us
  waiting for transfers between devices  71.2 us (37%)
  Pallas kernels  52.2 us (27%)
  starting transfers between devices  25.3 us (13%)
  blocking collectives  24.7 us (13%)
  local copies, waits for them, and re-layouts  14.3 us (7%)
  other arithmetic  6.27 us (3%)
    all_to_all x1, waiting for transfers between devices, body(): x = lax.all_to_all(x, 'seq', split_axis=0, concat_axis=0, tiled=True)  54.1 us
    pallas_call x1, Pallas kernels, ttt(): pl.pallas_call(ttt_kernel, out_shape=jax.ShapeDtypeStruct((x.shape[0], nh...  51.2 us
    all_to_all x1, blocking collectives, body(): y = lax.all_to_all(y, 'seq', split_axis=0, concat_axis=0, tiled=True)  24.7 us
    all_to_all x1, waiting for transfers between devices, body(): lax.all_to_all(packed, 'branch', split_axis=0, concat_axis=0, tiled=True)  14.7 us
    all_to_all x1, starting transfers between devices, body(): lax.all_to_all(packed, 'branch', split_axis=0, concat_axis=0, tiled=True)  11.6 us
    all_to_all x1, starting transfers between devices, body(): x = lax.all_to_all(x, 'seq', split_axis=0, concat_axis=0, tiled=True)  9.9 us
    transpose x3, local copies, waits for them, and re-layouts, by_group(): return x[0].T.reshape(groups, x.shape[2] // groups, tok)  6.89 us
  transfers between devices with their start and end apart: 3, of which 3 were waited for; matrix products, arithmetic and copies ran while one was open for 7% of the time, Pallas kernels for 0%

profile of v4, /device:TPU:1, one launch (start us, length us, event | category | flops | bytes accessed | tf_op | source)
XLA Modules:
  0.0 194.6 jit_solution(14146750442433136614)
XLA Ops:
  0.0 0.7 copy.27
  0.7 1.1 copy.21
  1.8 0.7 copy.28
  2.5 0.9 copy-done
  3.4 0.9 shard_map.118
  4.3 11.6 %all-to-all-start.1 = ((f32[16,8,896]{2,1,0:T(8,128)}), f32[16,8,896]{2,1,0:T(8,128)S(1)}, u32[]{:S(2)}, u32[]{:S(2)}) async-start(f32[16,8,896]{2,1,0:T(8,128)} %shard_map.118), calls=%async_computation.1 | async-start | bytes 917504 | tf_op jit(solution)/shard_map/all_to_all | solution.py:315
  15.9 0.7 compare_select_fusion
  16.6 14.7 %all-to-all-done.1 = f32[16,8,896]{2,1,0:T(8,128)S(1)} async-done(((f32[16,8,896]{2,1,0:T(8,128)}), f32[16,8,896]{2,1,0:T(8,128)S(1)}, u32[]{:S(2)}, u32[]{:S(2)}) %all-to-all-start.1) | async-done | bytes 458784 | tf_op jit(solution)/shard_map/all_to_all | solution.py:315
  31.3 1.4 gather_fusion
  32.7 3.8 %all-to-all-start.2 = ((f32[16,8,896]{2,1,0:T(8,128)}), f32[16,8,896]{2,1,0:T(8,128)S(1)}, u32[]{:S(2)}, u32[]{:S(2)}) async-start(f32[16,8,896]{2,1,0:T(8,128)} %gather_fusion), calls=%async_computation.2 | async-start | bytes 917504 | tf_op jit(solution)/shard_map/all_to_all | solution.py:317
  36.5 0.8 reshape.35
  37.3 1.7 copy.20
  39.0 2.6 %copy.19 = bf16[3072,256]{1,0:T(8,128)(2,1)} copy(bf16[3072,256]{0,1:T(8,128)(2,1)} %bitcast.38) | data formatting | bytes 3145728 | tf_op jit(solution)/shard_map/transpose | solution.py:323
  41.5 2.6 %copy.18 = bf16[3072,256]{1,0:T(8,128)(2,1)} copy(bf16[3072,256]{0,1:T(8,128)(2,1)} %bitcast.39) | data formatting | bytes 3145728 | tf_op jit(solution)/shard_map/transpose | solution.py:323
  44.2 3.7 %fusion.1 = bf16[16,592,256]{2,1,0:T(8,128)(2,1)} fusion(bf16[16,3,256]{2,1,0:T(4,128)(2,1)S(1)} %reshape.35, bf16[16,192,256]{2,1,0:T(8,128)(2,1)S(1)} %bitcast.33, bf16[16,192,256]{2,1,0:T(8,128)(2,1)} %bitcast.34, bf16[16,192,256]{2,1,0:T(8,128)(2,1)} %bitcast.35), kind=kLoop, calls=%fused_computation.3 | loop fusion | flops 24248320 | bytes 9592832 | tf_op jit(solution)/shard_map/concatenate | solution.py:326
  47.9 2.3 %all-to-all-done.2.own_ref = f32[16,8,896]{2,1,0:T(8,128)S(1)} async-done(((f32[16,8,896]{2,1,0:T(8,128)}), f32[16,8,896]{2,1,0:T(8,128)S(1)}, u32[]{:S(2)}, u32[]{:S(2)}) %all-to-all-start.2) | async-done | bytes 458784 | tf_op jit(solution)/shard_map/all_to_all | solution.py:317
  50.1 9.9 %all-to-all-start = ((bf16[16,592,256]{2,1,0:T(8,128)(2,1)}), bf16[16,592,256]{2,1,0:T(8,128)(2,1)}, u32[]{:S(2)}, u32[]{:S(2)}) async-start(bf16[16,592,256]{2,1,0:T(8,128)(2,1)} %fusion.1), calls=%async_computation | async-start | bytes 9699328 | tf_op jit(solution)/shard_map/all_to_all | solution.py:327
  60.7 1.9 multiply_sine_fusion
  62.6 54.1 %all-to-all-done.x_ref = bf16[16,592,256]{2,1,0:T(8,128)(2,1)} async-done(((bf16[16,592,256]{2,1,0:T(8,128)(2,1)}), bf16[16,592,256]{2,1,0:T(8,128)(2,1)}, u32[]{:S(2)}, u32[]{:S(2)}) %all-to-all-start) | async-done | bytes 4849696 | tf_op jit(solution)/shard_map/all_to_all | solution.py:327
  116.8 0.1 broadcast_in_dim.8.gain_ref
  116.9 0.1 broadcast_in_dim.9.shift_ref
  116.9 51.2 %shard_map.119 = bf16[16,192,256]{2,1,0:T(8,128)(2,1)S(1)} custom-call(bf16[16,592,256]{2,1,0:T(8,128)(2,1)} %all-to-all-done.x_ref, f32[16,32,256]{2,1,0:T(8,128)S(1)} %get-tuple-element.6.cos_ref, f32[16,32,256]{2,1,0:T(8,128)S(1)} %get-tuple-element.5.sin_ref, f32[3,64,128]{2,1,0:T(8,128)S(1)} %broadcast_in_dim.8.gain_ref, ...), custom_call_target="tpu_custom_call" | custom-call | tf_op jit(solution)/shard_map/pallas_call | solution.py:237
  168.2 24.7 %all_to_all.20 = bf16[16,192,256]{2,1,0:T(8,128)(2,1)S(1)} all-to-all(bf16[16,192,256]{2,1,0:T(8,128)(2,1)S(1)} %shard_map.119), channel_id=1, replica_groups=mesh['branch'=16,'seq'=16] {'seq'}, dimensions={0} | all-to-all | bytes 3145728 | tf_op jit(solution)/shard_map/all_to_all | solution.py:330
  192.9 1.7 copy.22
  (8 shorter events, 0.0 us)
Async XLA Ops:
  2.5 0.9 copy-start
  4.3 27.0 %all-to-all-start.1 = ((f32[16,8,896]{2,1,0:T(8,128)}), f32[16,8,896]{2,1,0:T(8,128)S(1)}, u32[]{:S(2)}, u32[]{:S(2)}) async-start(f32[16,8,896]{2,1,0:T(8,128)} %shard_map.118), calls=%async_computation.1 | async-start | bytes 917504 | tf_op jit(solution)/shard_map/all_to_all | solution.py:315
  32.7 17.5 %all-to-all-start.2 = ((f32[16,8,896]{2,1,0:T(8,128)}), f32[16,8,896]{2,1,0:T(8,128)S(1)}, u32[]{:S(2)}, u32[]{:S(2)}) async-start(f32[16,8,896]{2,1,0:T(8,128)} %gather_fusion), calls=%async_computation.2 | async-start | bytes 917504 | tf_op jit(solution)/shard_map/all_to_all | solution.py:317
  47.8 68.9 %copy-start.1 = (f32[3,64]{1,0:T(4,128)S(1)}, f32[3,64]{1,0:T(4,128)}, u32[]{:S(2)}) copy-start(f32[3,64]{1,0:T(4,128)} %param.16) | copy-start | bytes 2308
  47.9 69.0 %copy-start.2 = (f32[3,64]{1,0:T(4,128)S(1)}, f32[3,64]{1,0:T(4,128)}, u32[]{:S(2)}) copy-start(f32[3,64]{1,0:T(4,128)} %param.17) | copy-start | bytes 2308
  50.1 66.6 %all-to-all-start = ((bf16[16,592,256]{2,1,0:T(8,128)(2,1)}), bf16[16,592,256]{2,1,0:T(8,128)(2,1)}, u32[]{:S(2)}, u32[]{:S(2)}) async-start(bf16[16,592,256]{2,1,0:T(8,128)(2,1)} %fusion.1), calls=%async_computation | async-start | bytes 9699328 | tf_op jit(solution)/shard_map/all_to_all | solution.py:327

commit v5 on v4

--- a/solution.py
+++ b/solution.py
@@ -155,8 +155,7 @@
             v["dz"] = rstd * rate * ((g2c - m2) * rstd + target - c * e)
 
         def s_t(h, v):
-            hi, lo = tokmajor(v["dz"])
-            v["dzt"] = jnp.concatenate([hi[sl], lo[sl]], 1)
+            v["dzt"] = jnp.concatenate([jnp.transpose(jnp.concatenate([x, x], 0))[sl] for x in split(v["dz"])], 1)
 
         def s_da(h, v):
             v["da"] = dot(v["dzt"], stack4(*v["w2"], 0))
@@ -259,27 +258,26 @@
 
 
 def pack_kernel(w1_ref, c1_ref, w2_ref, c2_ref, out_ref):
-    nh = w1_ref.shape[0]
-    c1, c2 = c1_ref[...], c2_ref[...]
+    nh = w1_ref.shape[1]
+    c1 = jnp.concatenate([c1_ref[h] for h in range(nh)], 0)
     for h in range(nh):
         hl = slice(h * 256, h * 256 + 256)
-        w2 = jnp.transpose(w2_ref[h])
         for i in range(8):
-            out_ref[i, :, hl] = w1_ref[h, i * 8:i * 8 + 8]
-            out_ref[8 + i, :, hl] = w2[i * 8:i * 8 + 8]
+            out_ref[i, :, hl] = w1_ref[0, h, i * 8:i * 8 + 8]
+            out_ref[8 + i, :, hl] = w2_ref[0, h, i * 8:i * 8 + 8]
     out_ref[:, :, nh * 256:] = jnp.zeros_like(out_ref[:, :, nh * 256:])
     for i in range(16):
         out_ref[i, :nh, nh * 256:] = c1[:, :128]
         out_ref[i, nh:2 * nh, nh * 256:] = c1[:, 128:]
         for h in range(nh):
             at = nh * 256 + h % 2 * 64
-            out_ref[i, 2 * nh + h // 2:2 * nh + h // 2 + 1, at:at + 64] = c2[h:h + 1]
+            out_ref[i, 2 * nh + h // 2:2 * nh + h // 2 + 1, at:at + 64] = c2_ref[h]
 
 
 def pack(w1, c1, w2, c2):
     return pl.pallas_call(
         pack_kernel,
-        out_shape=jax.ShapeDtypeStruct((16, 8, w1.shape[0] * 256 + 128), f32),
+        out_shape=jax.ShapeDtypeStruct((16, 8, w1.shape[1] * 256 + 128), f32),
         in_specs=[pl.BlockSpec(memory_space=pltpu.VMEM)] * 4,
         out_specs=pl.BlockSpec(memory_space=pltpu.VMEM),
         compiler_params=pltpu.CompilerParams(vmem_limit_bytes=16 * 1024 * 1024),
@@ -311,7 +309,7 @@
     groups = lax.axis_size("seq")
     nh, tok = first_weight.shape[1], query_proj.shape[1]
 
-    packed = pack(first_weight[0], first_bias[0], second_weight[0], second_bias[0])
+    packed = pack(first_weight, jnp.swapaxes(first_bias, 0, 1), jnp.swapaxes(second_weight, 2, 3), jnp.swapaxes(second_bias, 0, 1))
     held = lax.all_to_all(packed, "branch", split_axis=0, concat_axis=0, tiled=True)
     picked = held.at[owner_map].get(mode="promise_in_bounds")
     own = lax.all_to_all(picked, "branch", split_axis=0, concat_axis=0, tiled=True)

time: 195 us -> 194 us (level)
  no operation moved by 1% of the time
where the time goes in v5:
time: 194 us; the launch traced here: 193 us
  waiting for transfers between devices  71.2 us (37%)
  Pallas kernels  51.1 us (26%)
  starting transfers between devices  25.3 us (13%)
  blocking collectives  24.7 us (13%)
  local copies, waits for them, and re-layouts  14.1 us (7%)
  other arithmetic  6.26 us (3%)
    all_to_all x1, waiting for transfers between devices, body(): x = lax.all_to_all(x, 'seq', split_axis=0, concat_axis=0, tiled=True)  54.1 us
    pallas_call x1, Pallas kernels, ttt(): pl.pallas_call(ttt_kernel, out_shape=jax.ShapeDtypeStruct((x.shape[0], nh...  50.3 us
    all_to_all x1, blocking collectives, body(): y = lax.all_to_all(y, 'seq', split_axis=0, concat_axis=0, tiled=True)  24.7 us
    all_to_all x1, waiting for transfers between devices, body(): lax.all_to_all(packed, 'branch', split_axis=0, concat_axis=0, tiled=True)  14.7 us
    all_to_all x1, starting transfers between devices, body(): lax.all_to_all(packed, 'branch', split_axis=0, concat_axis=0, tiled=True)  11.6 us
    all_to_all x1, starting transfers between devices, body(): x = lax.all_to_all(x, 'seq', split_axis=0, concat_axis=0, tiled=True)  9.9 us
    transpose x3, local copies, waits for them, and re-layouts, by_group(): return x[0].T.reshape(groups, x.shape[2] // groups, tok)  6.89 us
  transfers between devices with their start and end apart: 3, of which 3 were waited for; matrix products, arithmetic and copies ran while one was open for 7% of the time, Pallas kernels for 0%

profile of v5, /device:TPU:1, one launch (start us, length us, event | category | flops | bytes accessed | tf_op | source)
XLA Modules:
  0.0 193.4 jit_solution(4464808869040580313)
XLA Ops:
  0.0 0.9 copy-done
  0.9 0.9 copy-done.1
  1.9 0.7 copy-done.2
  2.5 0.7 copy-done.3
  3.2 0.8 shard_map.118
  4.1 11.6 %all-to-all-start.1 = ((f32[16,8,896]{2,1,0:T(8,128)}), f32[16,8,896]{2,1,0:T(8,128)S(1)}, u32[]{:S(2)}, u32[]{:S(2)}) async-start(f32[16,8,896]{2,1,0:T(8,128)} %shard_map.118), calls=%async_computation.1 | async-start | bytes 917504 | tf_op jit(solution)/shard_map/all_to_all | solution.py:313
  15.7 0.7 compare_select_fusion
  16.3 14.7 %all-to-all-done.1 = f32[16,8,896]{2,1,0:T(8,128)S(1)} async-done(((f32[16,8,896]{2,1,0:T(8,128)}), f32[16,8,896]{2,1,0:T(8,128)S(1)}, u32[]{:S(2)}, u32[]{:S(2)}) %all-to-all-start.1) | async-done | bytes 458784 | tf_op jit(solution)/shard_map/all_to_all | solution.py:313
  31.1 1.4 gather_fusion
  32.4 3.8 %all-to-all-start.2 = ((f32[16,8,896]{2,1,0:T(8,128)}), f32[16,8,896]{2,1,0:T(8,128)S(1)}, u32[]{:S(2)}, u32[]{:S(2)}) async-start(f32[16,8,896]{2,1,0:T(8,128)} %gather_fusion), calls=%async_computation.2 | async-start | bytes 917504 | tf_op jit(solution)/shard_map/all_to_all | solution.py:315
  36.2 0.8 reshape.35
  37.0 1.7 copy.19
  38.7 2.6 %copy.18 = bf16[3072,256]{1,0:T(8,128)(2,1)} copy(bf16[3072,256]{0,1:T(8,128)(2,1)} %bitcast.32) | data formatting | bytes 3145728 | tf_op jit(solution)/shard_map/transpose | solution.py:321
  41.3 2.6 %copy.17 = bf16[3072,256]{1,0:T(8,128)(2,1)} copy(bf16[3072,256]{0,1:T(8,128)(2,1)} %bitcast.33) | data formatting | bytes 3145728 | tf_op jit(solution)/shard_map/transpose | solution.py:321
  43.9 3.7 %fusion.1 = bf16[16,592,256]{2,1,0:T(8,128)(2,1)} fusion(bf16[16,3,256]{2,1,0:T(4,128)(2,1)S(1)} %reshape.35, bf16[16,192,256]{2,1,0:T(8,128)(2,1)S(1)} %bitcast.27, bf16[16,192,256]{2,1,0:T(8,128)(2,1)} %bitcast.28, bf16[16,192,256]{2,1,0:T(8,128)(2,1)} %bitcast.29), kind=kLoop, calls=%fused_computation.3 | loop fusion | flops 24248320 | bytes 9592832 | tf_op jit(solution)/shard_map/concatenate | solution.py:324
  47.6 2.3 %all-to-all-done.2.own_ref = f32[16,8,896]{2,1,0:T(8,128)S(1)} async-done(((f32[16,8,896]{2,1,0:T(8,128)}), f32[16,8,896]{2,1,0:T(8,128)S(1)}, u32[]{:S(2)}, u32[]{:S(2)}) %all-to-all-start.2) | async-done | bytes 458784 | tf_op jit(solution)/shard_map/all_to_all | solution.py:315
  49.9 9.9 %all-to-all-start = ((bf16[16,592,256]{2,1,0:T(8,128)(2,1)}), bf16[16,592,256]{2,1,0:T(8,128)(2,1)}, u32[]{:S(2)}, u32[]{:S(2)}) async-start(bf16[16,592,256]{2,1,0:T(8,128)(2,1)} %fusion.1), calls=%async_computation | async-start | bytes 9699328 | tf_op jit(solution)/shard_map/all_to_all | solution.py:325
  60.5 1.9 multiply_sine_fusion
  62.4 54.1 %all-to-all-done.x_ref = bf16[16,592,256]{2,1,0:T(8,128)(2,1)} async-done(((bf16[16,592,256]{2,1,0:T(8,128)(2,1)}), bf16[16,592,256]{2,1,0:T(8,128)(2,1)}, u32[]{:S(2)}, u32[]{:S(2)}) %all-to-all-start) | async-done | bytes 4849696 | tf_op jit(solution)/shard_map/all_to_all | solution.py:325
  116.5 0.1 broadcast_in_dim.8.gain_ref
  116.6 0.1 broadcast_in_dim.9.shift_ref
  116.7 50.3 %shard_map.119 = bf16[16,192,256]{2,1,0:T(8,128)(2,1)S(1)} custom-call(bf16[16,592,256]{2,1,0:T(8,128)(2,1)} %all-to-all-done.x_ref, f32[16,32,256]{2,1,0:T(8,128)S(1)} %get-tuple-element.6.cos_ref, f32[16,32,256]{2,1,0:T(8,128)S(1)} %get-tuple-element.5.sin_ref, f32[3,64,128]{2,1,0:T(8,128)S(1)} %broadcast_in_dim.8.gain_ref, ...), custom_call_target="tpu_custom_call" | custom-call | tf_op jit(solution)/shard_map/pallas_call | solution.py:236
  166.9 24.7 %all_to_all.20 = bf16[16,192,256]{2,1,0:T(8,128)(2,1)S(1)} all-to-all(bf16[16,192,256]{2,1,0:T(8,128)(2,1)S(1)} %shard_map.119), channel_id=1, replica_groups=mesh['branch'=16,'seq'=16] {'seq'}, dimensions={0} | all-to-all | bytes 3145728 | tf_op jit(solution)/shard_map/all_to_all | solution.py:328
  191.7 1.7 copy.20
  (11 shorter events, 0.0 us)
Async XLA Ops:
  0.0 0.9 copy-start
  0.9 0.9 copy-start.1
  1.9 0.7 copy-start.2
  2.5 0.7 copy-start.3
  4.1 27.0 %all-to-all-start.1 = ((f32[16,8,896]{2,1,0:T(8,128)}), f32[16,8,896]{2,1,0:T(8,128)S(1)}, u32[]{:S(2)}, u32[]{:S(2)}) async-start(f32[16,8,896]{2,1,0:T(8,128)} %shard_map.118), calls=%async_computation.1 | async-start | bytes 917504 | tf_op jit(solution)/shard_map/all_to_all | solution.py:313
  32.4 17.5 %all-to-all-start.2 = ((f32[16,8,896]{2,1,0:T(8,128)}), f32[16,8,896]{2,1,0:T(8,128)S(1)}, u32[]{:S(2)}, u32[]{:S(2)}) async-start(f32[16,8,896]{2,1,0:T(8,128)} %gather_fusion), calls=%async_computation.2 | async-start | bytes 917504 | tf_op jit(solution)/shard_map/all_to_all | solution.py:315
  47.6 68.9 %copy-start.4 = (f32[3,64]{1,0:T(4,128)S(1)}, f32[3,64]{1,0:T(4,128)}, u32[]{:S(2)}) copy-start(f32[3,64]{1,0:T(4,128)} %param.16) | copy-start | bytes 2308
  47.6 69.0 %copy-start.5 = (f32[3,64]{1,0:T(4,128)S(1)}, f32[3,64]{1,0:T(4,128)}, u32[]{:S(2)}) copy-start(f32[3,64]{1,0:T(4,128)} %param.17) | copy-start | bytes 2308
  49.9 66.6 %all-to-all-start = ((bf16[16,592,256]{2,1,0:T(8,128)(2,1)}), bf16[16,592,256]{2,1,0:T(8,128)(2,1)}, u32[]{:S(2)}, u32[]{:S(2)}) async-start(bf16[16,592,256]{2,1,0:T(8,128)(2,1)} %fusion.1), calls=%async_computation | async-start | bytes 9699328 | tf_op jit(solution)/shard_map/all_to_all | solution.py:325

commit v6 on v5

--- a/solution.py
+++ b/solution.py
@@ -280,7 +280,7 @@
         out_shape=jax.ShapeDtypeStruct((16, 8, w1.shape[1] * 256 + 128), f32),
         in_specs=[pl.BlockSpec(memory_space=pltpu.VMEM)] * 4,
         out_specs=pl.BlockSpec(memory_space=pltpu.VMEM),
-        compiler_params=pltpu.CompilerParams(vmem_limit_bytes=16 * 1024 * 1024),
+        compiler_params=pltpu.CompilerParams(vmem_limit_bytes=48 * 1024 * 1024),
     )(w1, c1, w2, c2)
 
 

time: 194 us -> 194 us (level)
  no operation moved by 1% of the time
where the time goes in v6:
time: 194 us; the launch traced here: 193 us
  waiting for transfers between devices  71.2 us (37%)
  Pallas kernels  51.1 us (26%)
  starting transfers between devices  25.3 us (13%)
  blocking collectives  24.7 us (13%)
  local copies, waits for them, and re-layouts  14.1 us (7%)
  other arithmetic  6.26 us (3%)
    all_to_all x1, waiting for transfers between devices, body(): x = lax.all_to_all(x, 'seq', split_axis=0, concat_axis=0, tiled=True)  54.1 us
    pallas_call x1, Pallas kernels, ttt(): pl.pallas_call(ttt_kernel, out_shape=jax.ShapeDtypeStruct((x.shape[0], nh...  50.3 us
    all_to_all x1, blocking collectives, body(): y = lax.all_to_all(y, 'seq', split_axis=0, concat_axis=0, tiled=True)  24.7 us
    all_to_all x1, waiting for transfers between devices, body(): lax.all_to_all(packed, 'branch', split_axis=0, concat_axis=0, tiled=True)  14.7 us
    all_to_all x1, starting transfers between devices, body(): lax.all_to_all(packed, 'branch', split_axis=0, concat_axis=0, tiled=True)  11.6 us
    all_to_all x1, starting transfers between devices, body(): x = lax.all_to_all(x, 'seq', split_axis=0, concat_axis=0, tiled=True)  9.9 us
    transpose x3, local copies, waits for them, and re-layouts, by_group(): return x[0].T.reshape(groups, x.shape[2] // groups, tok)  6.89 us
  transfers between devices with their start and end apart: 3, of which 3 were waited for; matrix products, arithmetic and copies ran while one was open for 7% of the time, Pallas kernels for 0%

profile of v6, /device:TPU:1, one launch (start us, length us, event | category | flops | bytes accessed | tf_op | source)
XLA Modules:
  0.0 193.4 jit_solution(1026227998375568450)
XLA Ops:
  0.0 0.9 copy-done
  0.9 0.9 copy-done.1
  1.9 0.7 copy-done.2
  2.5 0.7 copy-done.3
  3.2 0.8 shard_map.118
  4.1 11.6 %all-to-all-start.1 = ((f32[16,8,896]{2,1,0:T(8,128)}), f32[16,8,896]{2,1,0:T(8,128)S(1)}, u32[]{:S(2)}, u32[]{:S(2)}) async-start(f32[16,8,896]{2,1,0:T(8,128)} %shard_map.118), calls=%async_computation.1 | async-start | bytes 917504 | tf_op jit(solution)/shard_map/all_to_all | solution.py:313
  15.7 0.7 compare_select_fusion
  16.3 14.7 %all-to-all-done.1 = f32[16,8,896]{2,1,0:T(8,128)S(1)} async-done(((f32[16,8,896]{2,1,0:T(8,128)}), f32[16,8,896]{2,1,0:T(8,128)S(1)}, u32[]{:S(2)}, u32[]{:S(2)}) %all-to-all-start.1) | async-done | bytes 458784 | tf_op jit(solution)/shard_map/all_to_all | solution.py:313
  31.1 1.4 gather_fusion
  32.4 3.8 %all-to-all-start.2 = ((f32[16,8,896]{2,1,0:T(8,128)}), f32[16,8,896]{2,1,0:T(8,128)S(1)}, u32[]{:S(2)}, u32[]{:S(2)}) async-start(f32[16,8,896]{2,1,0:T(8,128)} %gather_fusion), calls=%async_computation.2 | async-start | bytes 917504 | tf_op jit(solution)/shard_map/all_to_all | solution.py:315
  36.2 0.8 reshape.35
  37.0 1.7 copy.19
  38.7 2.6 %copy.18 = bf16[3072,256]{1,0:T(8,128)(2,1)} copy(bf16[3072,256]{0,1:T(8,128)(2,1)} %bitcast.32) | data formatting | bytes 3145728 | tf_op jit(solution)/shard_map/transpose | solution.py:321
  41.3 2.6 %copy.17 = bf16[3072,256]{1,0:T(8,128)(2,1)} copy(bf16[3072,256]{0,1:T(8,128)(2,1)} %bitcast.33) | data formatting | bytes 3145728 | tf_op jit(solution)/shard_map/transpose | solution.py:321
  43.9 3.7 %fusion.1 = bf16[16,592,256]{2,1,0:T(8,128)(2,1)} fusion(bf16[16,3,256]{2,1,0:T(4,128)(2,1)S(1)} %reshape.35, bf16[16,192,256]{2,1,0:T(8,128)(2,1)S(1)} %bitcast.27, bf16[16,192,256]{2,1,0:T(8,128)(2,1)} %bitcast.28, bf16[16,192,256]{2,1,0:T(8,128)(2,1)} %bitcast.29), kind=kLoop, calls=%fused_computation.3 | loop fusion | flops 24248320 | bytes 9592832 | tf_op jit(solution)/shard_map/concatenate | solution.py:324
  47.6 2.3 %all-to-all-done.2.own_ref = f32[16,8,896]{2,1,0:T(8,128)S(1)} async-done(((f32[16,8,896]{2,1,0:T(8,128)}), f32[16,8,896]{2,1,0:T(8,128)S(1)}, u32[]{:S(2)}, u32[]{:S(2)}) %all-to-all-start.2) | async-done | bytes 458784 | tf_op jit(solution)/shard_map/all_to_all | solution.py:315
  49.9 9.9 %all-to-all-start = ((bf16[16,592,256]{2,1,0:T(8,128)(2,1)}), bf16[16,592,256]{2,1,0:T(8,128)(2,1)}, u32[]{:S(2)}, u32[]{:S(2)}) async-start(bf16[16,592,256]{2,1,0:T(8,128)(2,1)} %fusion.1), calls=%async_computation | async-start | bytes 9699328 | tf_op jit(solution)/shard_map/all_to_all | solution.py:325
  60.5 1.9 multiply_sine_fusion
  62.4 54.1 %all-to-all-done.x_ref = bf16[16,592,256]{2,1,0:T(8,128)(2,1)} async-done(((bf16[16,592,256]{2,1,0:T(8,128)(2,1)}), bf16[16,592,256]{2,1,0:T(8,128)(2,1)}, u32[]{:S(2)}, u32[]{:S(2)}) %all-to-all-start) | async-done | bytes 4849696 | tf_op jit(solution)/shard_map/all_to_all | solution.py:325
  116.5 0.1 broadcast_in_dim.8.gain_ref
  116.6 0.1 broadcast_in_dim.9.shift_ref
  116.7 50.3 %shard_map.119 = bf16[16,192,256]{2,1,0:T(8,128)(2,1)S(1)} custom-call(bf16[16,592,256]{2,1,0:T(8,128)(2,1)} %all-to-all-done.x_ref, f32[16,32,256]{2,1,0:T(8,128)S(1)} %get-tuple-element.6.cos_ref, f32[16,32,256]{2,1,0:T(8,128)S(1)} %get-tuple-element.5.sin_ref, f32[3,64,128]{2,1,0:T(8,128)S(1)} %broadcast_in_dim.8.gain_ref, ...), custom_call_target="tpu_custom_call" | custom-call | tf_op jit(solution)/shard_map/pallas_call | solution.py:236
  166.9 24.7 %all_to_all.20 = bf16[16,192,256]{2,1,0:T(8,128)(2,1)S(1)} all-to-all(bf16[16,192,256]{2,1,0:T(8,128)(2,1)S(1)} %shard_map.119), channel_id=1, replica_groups=mesh['branch'=16,'seq'=16] {'seq'}, dimensions={0} | all-to-all | bytes 3145728 | tf_op jit(solution)/shard_map/all_to_all | solution.py:328
  191.7 1.7 copy.20
  (11 shorter events, 0.0 us)
Async XLA Ops:
  0.0 0.9 copy-start
  0.9 0.9 copy-start.1
  1.9 0.7 copy-start.2
  2.5 0.7 copy-start.3
  4.1 27.0 %all-to-all-start.1 = ((f32[16,8,896]{2,1,0:T(8,128)}), f32[16,8,896]{2,1,0:T(8,128)S(1)}, u32[]{:S(2)}, u32[]{:S(2)}) async-start(f32[16,8,896]{2,1,0:T(8,128)} %shard_map.118), calls=%async_computation.1 | async-start | bytes 917504 | tf_op jit(solution)/shard_map/all_to_all | solution.py:313
  32.4 17.5 %all-to-all-start.2 = ((f32[16,8,896]{2,1,0:T(8,128)}), f32[16,8,896]{2,1,0:T(8,128)S(1)}, u32[]{:S(2)}, u32[]{:S(2)}) async-start(f32[16,8,896]{2,1,0:T(8,128)} %gather_fusion), calls=%async_computation.2 | async-start | bytes 917504 | tf_op jit(solution)/shard_map/all_to_all | solution.py:315
  47.6 68.9 %copy-start.4 = (f32[3,64]{1,0:T(4,128)S(1)}, f32[3,64]{1,0:T(4,128)}, u32[]{:S(2)}) copy-start(f32[3,64]{1,0:T(4,128)} %param.16) | copy-start | bytes 2308
  47.6 69.0 %copy-start.5 = (f32[3,64]{1,0:T(4,128)S(1)}, f32[3,64]{1,0:T(4,128)}, u32[]{:S(2)}) copy-start(f32[3,64]{1,0:T(4,128)} %param.17) | copy-start | bytes 2308
  49.9 66.6 %all-to-all-start = ((bf16[16,592,256]{2,1,0:T(8,128)(2,1)}), bf16[16,592,256]{2,1,0:T(8,128)(2,1)}, u32[]{:S(2)}, u32[]{:S(2)}) async-start(bf16[16,592,256]{2,1,0:T(8,128)(2,1)} %fusion.1), calls=%async_computation | async-start | bytes 9699328 | tf_op jit(solution)/shard_map/all_to_all | solution.py:325
